TPU v7x, 32 devices: a whole 2x2x4 slice. The times are simulated.
32 devices in a mesh: section: 2 (over core), dp: 16 (over z, y, x).
Axes of the slice: x: 2, y: 2, z: 4, core: 2. Of those that a mesh axis runs over, the one named last changes fastest.
Arguments:
- codebook_embed: bfloat16 [2, 2048, 3, 1024], P(None, 'dp'), may hold values from -6 to 6
- item_lengths: int32 [2, 16, 8], P(None, 'dp'), may hold values from 1 to 64, 128 in all within a row
- gain_attn: float32 [2, 1024], P('section'), may hold values from 0.5 to 1.5
- w_qkv: bfloat16 [2, 1024, 3072], P('section'), may hold values from -0.1875 to 0.1875
- w_out: bfloat16 [2, 1024, 1024], P('section'), may hold values from -0.375 to 0.375
- gain_mlp: float32 [2, 1024], P('section'), may hold values from 0.5 to 1.5
- w_up: bfloat16 [2, 1024, 4096], P('section'), may hold values from -0.1875 to 0.1875
- w_down: bfloat16 [2, 4096, 1024], P('section'), may hold values from -0.09375 to 0.09375
- cotangent: bfloat16 [2, 2048, 3, 1024], P(None, 'dp'), may hold values from -6 to 6
Outputs:
- local_out: bfloat16 [2, 2048, 3, 1024], P(None, 'dp', None, 'section')
- embed_grad: float32 [2, 2048, 3, 1024], P(None, 'dp', None, 'section')
- grad_gain_attn: float32 [2, 1024], P('section', 'dp')
- grad_w_qkv: float32 [2, 1024, 3072], P('section', 'dp')
- grad_w_out: float32 [2, 1024, 1024], P('section', 'dp')
- grad_gain_mlp: float32 [2, 1024], P('section', 'dp')
- grad_w_up: float32 [2, 1024, 4096], P('section', 'dp')
- grad_w_down: float32 [2, 4096, 1024], P('section', 'dp')
Inputs may be any that keep to these rules, and one draw needn't show every extreme that they name: `item_lengths`: for every micro-batch and index of dp the 8 lengths sum to 128 and the largest is exactly 64.
All inputs are finite; a program needn't handle non-finite values.
Results may differ from a plain program's by a relative error of at most 0.015.
Values may be sent and summed in bfloat16 or wider, within the bound.
No kernel may reach another device: no remote copies, remote signals or barrier semaphores. Data moves between devices by JAX's collectives and lax.ppermute only.
A program may use at most 576 MiB of HBM per device.

v0:
```python
import jax
import jax.numpy as jnp
from jax import lax
from jax.sharding import PartitionSpec as P

HEADS = 16


EPSILON = 1e-05


def passed_along(array, axis, by):
    length = lax.axis_size(axis)
    pairs = [(i, i + by) for i in range(length) if 0 <= i + by < length]
    return lax.ppermute(array, axis, pairs)


def normalize(layer_in, gain):
    return (
        layer_in * lax.rsqrt(jnp.mean(layer_in * layer_in, axis=-1, keepdims=True) + EPSILON) * gain
    )


def inner_left(left, right):
    return lax.dot_general(
        left, right, (((0,), (0,)), ((), ())), preferred_element_type=jnp.float32
    )


def inner_right(left, right):
    return lax.dot_general(
        left, right, (((1,), (1,)), ((), ())), preferred_element_type=jnp.float32
    )


def frame_mask(lengths, row_count):
    item_ends = jnp.cumsum(lengths)
    position = jnp.arange(row_count, dtype=jnp.int32)
    item_owner = jnp.sum((position[:, None] >= item_ends[None, :]).astype(jnp.int32), axis=1)
    same_item = item_owner[:, None] == item_owner[None, :]
    return (same_item & (position[:, None] >= position[None, :]))[None, None]


def code_mask(length):
    position = jnp.arange(length, dtype=jnp.int32)
    return (position[:, None] >= position[None, :])[None, None]


def empty_store(row_count, groups, features, hidden_width):
    return (
        jnp.zeros((row_count, features), jnp.bfloat16),
        jnp.zeros((row_count, 3 * features), jnp.bfloat16),
        jnp.zeros((groups, HEADS, row_count // groups, 1), jnp.float32),
        jnp.zeros((row_count, features), jnp.bfloat16),
        jnp.zeros((row_count, features), jnp.float32),
        jnp.zeros((row_count, features), jnp.bfloat16),
        jnp.zeros((row_count, hidden_width), jnp.float32),
        jnp.zeros((row_count, hidden_width), jnp.bfloat16),
    )


def attention_scores(queries, key_rows, allowed, head_width):
    scores = jnp.einsum(
        "gqhd,gkhd->ghqk", queries, key_rows, preferred_element_type=jnp.float32
    ) * head_width ** (-0.5)
    return jnp.where(allowed, scores, -1e30)


def block_forward(weight_set, layer_in, groups, allowed):
    gain_one, w_qkv, w_out, gain_two, w_up, w_down = weight_set
    row_count, features = layer_in.shape
    head_width = features // HEADS
    normed = normalize(layer_in, gain_one).astype(jnp.bfloat16)
    packed = jnp.dot(normed, w_qkv, preferred_element_type=jnp.float32).astype(jnp.bfloat16)
    shaped = packed.reshape(groups, row_count // groups, 3, HEADS, head_width)
    queries, key_rows, values = (shaped[:, :, 0], shaped[:, :, 1], shaped[:, :, 2])
    scores = attention_scores(queries, key_rows, allowed, head_width)
    row_peak = jnp.max(scores, axis=-1, keepdims=True)
    exponent = jnp.exp(scores - row_peak)
    row_total = jnp.sum(exponent, axis=-1, keepdims=True)
    attn_probs = (exponent / row_total).astype(jnp.bfloat16)
    mixture = jnp.einsum("ghqk,gkhd->gqhd", attn_probs, values, preferred_element_type=jnp.float32)
    mixture = mixture.reshape(row_count, features).astype(jnp.bfloat16)
    middle = layer_in + jnp.dot(mixture, w_out, preferred_element_type=jnp.float32)
    normed_two = normalize(middle, gain_two).astype(jnp.bfloat16)
    hidden = jnp.dot(normed_two, w_up, preferred_element_type=jnp.float32)
    active = jax.nn.gelu(hidden).astype(jnp.bfloat16)
    result = middle + jnp.dot(active, w_down, preferred_element_type=jnp.float32)
    stored = (
        normed,
        packed,
        row_peak + jnp.log(row_total),
        mixture,
        middle,
        normed_two,
        hidden,
        active,
    )
    return (result, stored)


def block_backward(weight_set, layer_in, groups, allowed, stored, grad_out):
    gain_one, w_qkv, w_out, gain_two, w_up, w_down = weight_set
    normed, packed, log_total, mixture, middle, normed_two, hidden, active = stored
    row_count, features = layer_in.shape
    head_width = features // HEADS
    low_out = grad_out.astype(jnp.bfloat16)
    grad_down = inner_left(active, low_out)
    grad_active = inner_right(low_out, w_down)
    gelu_back = jax.vjp(jax.nn.gelu, hidden)[1]
    grad_hidden = gelu_back(grad_active)[0].astype(jnp.bfloat16)
    grad_up = inner_left(normed_two, grad_hidden)
    norm_back = jax.vjp(normalize, middle, gain_two)[1]
    grad_middle, grad_gain_two = norm_back(inner_right(grad_hidden, w_up))
    grad_middle = grad_middle + grad_out
    low_middle = grad_middle.astype(jnp.bfloat16)
    grad_wout = inner_left(mixture, low_middle)
    grad_mixture = inner_right(low_middle, w_out).astype(jnp.bfloat16)
    grad_mixture = grad_mixture.reshape(groups, row_count // groups, HEADS, head_width)
    shaped = packed.reshape(groups, row_count // groups, 3, HEADS, head_width)
    queries, key_rows, values = (shaped[:, :, 0], shaped[:, :, 1], shaped[:, :, 2])
    attn_probs = jnp.exp(attention_scores(queries, key_rows, allowed, head_width) - log_total)
    grad_values = jnp.einsum(
        "ghqk,gqhd->gkhd",
        attn_probs.astype(jnp.bfloat16),
        grad_mixture,
        preferred_element_type=jnp.float32,
    )
    grad_probs = jnp.einsum(
        "gqhd,gkhd->ghqk", grad_mixture, values, preferred_element_type=jnp.float32
    )
    grad_scores = attn_probs * (
        grad_probs - jnp.sum(grad_probs * attn_probs, axis=-1, keepdims=True)
    )
    grad_scores = grad_scores.astype(jnp.bfloat16)
    scale_keys = head_width ** (-0.5)
    grad_queries = (
        jnp.einsum("ghqk,gkhd->gqhd", grad_scores, key_rows, preferred_element_type=jnp.float32)
        * scale_keys
    )
    grad_keys = (
        jnp.einsum("ghqk,gqhd->gkhd", grad_scores, queries, preferred_element_type=jnp.float32)
        * scale_keys
    )
    grad_packed = jnp.stack([grad_queries, grad_keys, grad_values], axis=2)
    grad_packed = grad_packed.reshape(row_count, 3 * features).astype(jnp.bfloat16)
    grad_qkv = inner_left(normed, grad_packed)
    norm_back_one = jax.vjp(normalize, layer_in, gain_one)[1]
    grad_in, grad_gain_one = norm_back_one(inner_right(grad_packed, w_qkv))
    return (
        grad_in + grad_middle,
        (grad_gain_one, grad_qkv, grad_wout, grad_gain_two, grad_up, grad_down),
    )


def add_terms(first, second):
    return tuple((left + right for left, right in zip(first, second)))


def local(codebook_embed, item_lengths, gain_attn, w_qkv, w_out, gain_mlp, w_up, w_down, cotangent):
    section_index = lax.axis_index("section")
    weight_set = (gain_attn[0], w_qkv[0], w_out[0], gain_mlp[0], w_up[0], w_down[0])
    micro_count, frames, books, features = codebook_embed.shape
    hidden_width = w_up.shape[2]
    local_mask = code_mask(books)
    scale_in = books ** (-0.5)
    state_zero = jnp.zeros((frames, features), jnp.bfloat16)
    grad_zero = tuple((jnp.zeros(matrix.shape, jnp.float32) for matrix in weight_set))
    contrib_zero = jnp.zeros((frames, books, features), jnp.float32)
    output_zero = jnp.zeros((frames, books, features), jnp.bfloat16)
    global_empty = empty_store(frames, 1, features, hidden_width)
    local_empty = empty_store(frames * books, frames, features, hidden_width)
    received_all = []
    output_all = []
    global_kept = []
    local_kept = []
    for micro in range(micro_count):
        embed_rows = codebook_embed[micro].astype(jnp.float32)
        global_mask = frame_mask(item_lengths[micro, 0], frames)

        def global_work():
            frame_out, stored = block_forward(
                weight_set, jnp.sum(embed_rows, axis=1) * scale_in, 1, global_mask
            )
            return (frame_out.astype(jnp.bfloat16), stored)

        sent_states, global_stored = lax.cond(
            section_index == 0, global_work, lambda: (state_zero, global_empty)
        )
        received = passed_along(sent_states, "section", 1)

        def local_work():
            local_in = (embed_rows + received.astype(jnp.float32)[:, None, :]).reshape(
                frames * books, features
            )
            layer_out, stored = block_forward(weight_set, local_in, frames, local_mask)
            return (layer_out.astype(jnp.bfloat16).reshape(frames, books, features), stored)

        local_result, local_stored = lax.cond(
            section_index == 1, local_work, lambda: (output_zero, local_empty)
        )
        output_all.append(local_result)
        received_all.append(received)
        global_kept.append(global_stored)
        local_kept.append(local_stored)
    layer_out = jnp.stack(output_all)
    half_width = features // 2
    other_half = passed_along(layer_out[..., :half_width], "section", -1)
    own_half = jnp.where(section_index == 0, other_half, layer_out[..., half_width:])
    embed_grads = []
    sum_list = []
    for micro in range(micro_count):
        embed_rows = codebook_embed[micro].astype(jnp.float32)
        global_mask = frame_mask(item_lengths[micro, 0], frames)
        received = received_all[micro]
        upstream = cotangent[micro].astype(jnp.float32).reshape(frames * books, features)

        def local_back():
            local_in = (embed_rows + received.astype(jnp.float32)[:, None, :]).reshape(
                frames * books, features
            )
            result, stored = block_forward(weight_set, local_in, frames, local_mask)
            grad_in, grad_terms = block_backward(
                weight_set, local_in, frames, local_mask, stored, upstream
            )
            grad_in = grad_in.reshape(frames, books, features)
            return (grad_in, jnp.sum(grad_in, axis=1).astype(jnp.bfloat16), grad_terms)

        local_grad, frame_grad, local_terms = lax.cond(
            section_index == 1, local_back, lambda: (contrib_zero, state_zero, grad_zero)
        )
        returned = passed_along(frame_grad, "section", -1)

        def global_back():
            frame_in = jnp.sum(embed_rows, axis=1) * scale_in
            result, stored = block_forward(weight_set, frame_in, 1, global_mask)
            grad_in, grad_terms = block_backward(
                weight_set, frame_in, 1, global_mask, stored, returned.astype(jnp.float32)
            )
            spread = jnp.broadcast_to((grad_in * scale_in)[:, None, :], (frames, books, features))
            return (spread, grad_terms)

        global_grad, global_terms = lax.cond(
            section_index == 0, global_back, lambda: (contrib_zero, grad_zero)
        )
        embed_grads.append(
            lax.psum_scatter(
                (local_grad + global_grad).astype(jnp.bfloat16),
                "section",
                scatter_dimension=2,
                tiled=True,
            ).astype(jnp.float32)
        )
        grad_terms = add_terms(local_terms, global_terms)
        sum_list.append(grad_terms)
    combined = sum_list[0]
    for extra in sum_list[1:]:
        combined = add_terms(combined, extra)
    reduced = (
        lax.psum_scatter(combined[0], "dp", scatter_dimension=0, tiled=True),
        lax.psum_scatter(combined[1], "dp", scatter_dimension=0, tiled=True),
        lax.psum_scatter(combined[2], "dp", scatter_dimension=0, tiled=True),
        lax.psum_scatter(combined[3], "dp", scatter_dimension=0, tiled=True),
        lax.psum_scatter(combined[4], "dp", scatter_dimension=0, tiled=True),
        lax.psum_scatter(combined[5], "dp", scatter_dimension=0, tiled=True),
    )
    return (
        own_half,
        jnp.stack(embed_grads),
        reduced[0][None],
        reduced[1][None],
        reduced[2][None],
        reduced[3][None],
        reduced[4][None],
        reduced[5][None],
    )


def solution(mesh):
    in_specs = (
        P(None, "dp", None, None),
        P(None, "dp", None),
        P("section", None),
        P("section", None, None),
        P("section", None, None),
        P("section", None),
        P("section", None, None),
        P("section", None, None),
        P(None, "dp", None, None),
    )
    out_specs = (
        P(None, "dp", None, "section"),
        P(None, "dp", None, "section"),
        P("section", "dp"),
        P("section", "dp", None),
        P("section", "dp", None),
        P("section", "dp"),
        P("section", "dp", None),
        P("section", "dp", None),
    )
    return jax.shard_map(local, mesh=mesh, in_specs=in_specs, out_specs=out_specs, check_vma=False)
```

profile of v0, /device:TPU:0, one launch (start us, length us, event | category | flops | bytes accessed | tf_op | source)
XLA Modules:
  0.0 1655.4 jit_solution(363906318991623958)
XLA Ops:
  15.3 25.0 %conditional.10 = (bf16[128,1024]{1,0:T(8,128)(2,1)S(1)}) conditional(s32[]{:T(128)} %convert_element_type.409, () %tuple.73, (f32[128,3,1024]{2,1,0:T(4,128)}, f32[1,1024]{1,0:T(1,128)S(1)}, bf16[1024,3072]{1,0:T(8,128)(2,1)}, pred[1,1,128,128]{2,3,1,0:T(8,128)(4,1)S(1)}, bf16[1024,1024]{1,0:T(8,128)(2,1)S(1)}, ...), branch_computations={%region_17.18_spmd, %region_18.24_spmd} | conditional | flops 3331721728 | bytes 37548044 | solution.py:187
  31.8 8.5 fusion.75
  44.3 23.7 %conditional.14 = (bf16[128,1024]{1,0:T(8,128)(2,1)S(1)}, f32[1024]{0:T(1024)S(1)}, f32[1024,3072]{1,0:T(8,128)}, f32[1024,1024]{1,0:T(8,128)}, f32[1024]{0:T(10...) conditional(s32[]{:T(128)} %convert_element_type.408, () %tuple.80, ...), branch_computations={%region_55.56_spmd, %region_56.67_spmd} | conditional | flops 25853990912 | bytes 364888224 | solution.py:229
  55.2 7.9 broadcast_in_dim.285
  69.3 183.9 %collective-permute-done.4 = bf16[128,1024]{1,0:T(8,128)(2,1)S(1)} collective-permute-done((bf16[128,1024]{1,0:T(8,128)(2,1)S(1)}, bf16[128,1024]{1,0:T(8,128)(2,1)S(1)}, u32[]{:S(2)}, u32[]{:S(2)}) %collective-permute-start.4) | collective-permute-done | bytes 262176 | tf_op jit(solution)/shard_map/ppermute | solution.py:15
  253.2 60.0 %conditional.15 = (f32[1024]{0:T(1024)S(1)}, f32[1024,3072]{1,0:T(8,128)}, f32[1024,1024]{1,0:T(8,128)S(1)}, f32[1024]{0:T(1024)S(1)}, f32[1024,4096]{1,0:T(8,12...) conditional(s32[]{:T(128)} %convert_element_type.409, () %tuple.82, (f32[128,3,1024]{2,1,0:T(4,128)}, ...), branch_computations={%region_67.68_spmd, %region_68.79_spmd} | conditional | flops 8819568640 | bytes 234796064 | solution.py:243
  303.1 8.1 fusion.245
  323.9 25.0 %conditional.8 = (bf16[128,1024]{1,0:T(8,128)(2,1)S(1)}) conditional(s32[]{:T(128)} %convert_element_type.409, () %tuple.69, (f32[128,3,1024]{2,1,0:T(4,128)}, f32[1,1024]{1,0:T(1,128)S(1)}, bf16[1024,3072]{1,0:T(8,128)(2,1)}, pred[1,1,128,128]{2,3,1,0:T(8,128)(4,1)S(1)}, bf16[1024,1024]{1,0:T(8,128)(2,1)S(1)}, /*index=5*/f32[1,1024]{1,0:T(1,128)S(1)}, ...), branch_computations={%region_2.3_spmd, %region_3.9_spmd} | conditional | flops 3331721728 | bytes 37548044 | solution.py:187
  340.4 8.5 fusion.12
  353.0 23.2 %conditional.12 = (bf16[128,1024]{1,0:T(8,128)(2,1)S(1)}, f32[1024]{0:T(1024)S(1)}, f32[1024,3072]{1,0:T(8,128)}, f32[1024,1024]{1,0:T(8,128)}, f32[1024]{0:T(10...) conditional(s32[]{:T(128)} %convert_element_type.408, () %tuple.76, ...), branch_computations={%region_30.31_spmd, %region_31.42_spmd} | conditional | flops 25853990912 | bytes 364888224 | solution.py:229
  377.5 175.9 %collective-permute-done.3 = bf16[128,1024]{1,0:T(8,128)(2,1)S(1)} collective-permute-done((bf16[128,1024]{1,0:T(8,128)(2,1)S(1)}, bf16[128,1024]{1,0:T(8,128)(2,1)S(1)}, u32[]{:S(2)}, u32[]{:S(2)}) %collective-permute-start.3) | collective-permute-done | bytes 262176 | tf_op jit(solution)/shard_map/ppermute | solution.py:15
  553.5 67.3 %conditional.13 = (f32[1024]{0:T(1024)S(1)}, f32[1024,3072]{1,0:T(8,128)}, f32[1024,1024]{1,0:T(8,128)}, f32[1024]{0:T(1024)S(1)}, f32[1024,4096]{1,0:T(8,128)},...) conditional(s32[]{:T(128)} %convert_element_type.409, () %tuple.78, (f32[128,3,1024]{2,1,0:T(4,128)}, ...), branch_computations={%region_42.43_spmd, %region_43.54_spmd} | conditional | flops 8819568640 | bytes 234796064 | solution.py:243
  602.6 8.2 fusion.196
  610.8 8.2 fusion.173
  623.9 10.3 add_add_fusion.11
  634.3 23.3 %add_add_fusion.10 = f32[1024,3072]{1,0:T(8,128)} fusion(f32[1024,3072]{1,0:T(8,128)} %get-tuple-element.286, f32[1024,3072]{1,0:T(8,128)} %get-tuple-element.287, f32[1024,3072]{1,0:T(8,128)} %get-tuple-element.284, f32[1024,3072]{1,0:T(8,128)} %get-tuple-element.285), kind=kLoop, calls=%fused_computation.468 | loop fusion | flops 9437184 | bytes 62914560 | tf_op jit(solution)/shard_map/add | solution.py:157
  657.7 29.0 %add_add_fusion.9 = f32[1024,4096]{1,0:T(8,128)} fusion(f32[1024,4096]{1,0:T(8,128)} %copy-done.7, f32[1024,4096]{1,0:T(8,128)} %copy-done.9, f32[1024,4096]{1,0:T(8,128)} %get-tuple-element.296, f32[1024,4096]{1,0:T(8,128)} %get-tuple-element.297), kind=kLoop, calls=%fused_computation.467 | loop fusion | flops 12582912 | bytes 83886080 | tf_op jit(solution)/shard_map/add | solution.py:157
  686.8 29.7 %add_add_fusion.8 = f32[4096,1024]{1,0:T(8,128)} fusion(f32[4096,1024]{1,0:T(8,128)} %get-tuple-element.302, f32[4096,1024]{1,0:T(8,128)} %get-tuple-element.303, f32[4096,1024]{1,0:T(8,128)} %copy-done.8, f32[4096,1024]{1,0:T(8,128)} %get-tuple-element.301), kind=kLoop, calls=%fused_computation.466 | loop fusion | flops 12582912 | bytes 83886080 | tf_op jit(solution)/shard_map/add | solution.py:157
  718.1 10.2 conditional.9
  739.1 45.9 %all-reduce.2 = (f32[1024]{0:T(1024)S(1)}, f32[1024]{0:T(1024)S(1)}) all-reduce(f32[1024]{0:T(1024)S(1)} %add_add_fusion.13, f32[1024]{0:T(1024)S(1)} %add_add_fusion.12), channel_id=4, replica_groups=mesh['section'=2,'dp'=16] {'dp'}, use_global_device_ids=true, to_apply=%region_80.81.clone | all-reduce | flops 2048 | bytes 16384
  786.3 41.1 %collective-permute-done.2 = bf16[2,128,3,512]{3,1,2,0:T(8,128)(2,1)S(1)} collective-permute-done((bf16[2,128,3,512]{3,1,2,0:T(8,128)(2,1)S(1)}, bf16[2,128,3,512]{3,1,2,0:T(8,128)(2,1)S(1)}, u32[]{:S(2)}, u32[]{:S(2)}) %collective-permute-start.2) | collective-permute-done | bytes 786464 | tf_op jit(solution)/shard_map/ppermute | solution.py:15
  830.7 113.9 %reduce-scatter.11.cloned.1.call-done = f32[64,3072]{1,0:T(8,128)} async-done(((f32[1024,3072]{1,0:T(8,128)}), f32[64,3072]{1,0:T(8,128)}) %reduce-scatter.11.cloned.1.call-update) | async-done | bytes 786448 | tf_op jit(solution)/shard_map/reduce_scatter | solution.py:261
  944.6 348.9 %reduce-scatter.15.cloned.1.call-done = f32[64,4096]{1,0:T(8,128)} async-done(((f32[1024,4096]{1,0:T(8,128)}), f32[64,4096]{1,0:T(8,128)}) %reduce-scatter.15.cloned.1.call-update) | async-done | bytes 1048592 | tf_op jit(solution)/shard_map/reduce_scatter | solution.py:264
  1293.4 354.9 %reduce-scatter.17.cloned.1.call-done = f32[256,1024]{1,0:T(8,128)} async-done(((f32[4096,1024]{1,0:T(8,128)}), f32[256,1024]{1,0:T(8,128)}) %reduce-scatter.17.cloned.1.call-update) | async-done | bytes 1048592 | tf_op jit(solution)/shard_map/reduce_scatter | solution.py:265
  (277 shorter events, 215.7 us)
Async XLA Ops:
  7.2 821.1 %reduce-scatter.9.cloned.1.call-start = ((), (), s32[]{:S(2)}) async-start(), calls=%async_computation.7 | async-start | bytes 1179648 | tf_op jit(solution)/shard_map/reduce_scatter | solution.py:247
  41.0 2.6 collective-permute-start.1
  68.0 185.2 %copy-start.7 = (f32[1024,4096]{1,0:T(8,128)}, f32[1024,4096]{1,0:T(8,128)S(1)}, u32[]{:S(2)}) copy-start(f32[1024,4096]{1,0:T(8,128)S(1)} %get-tuple-element.298) | copy-start | bytes 50331652
  68.0 185.2 %copy-start.66 = (f32[1024]{0:T(1024)}, f32[1024]{0:T(1024)S(1)}, u32[]{:S(2)}) copy-start(f32[1024]{0:T(1024)S(1)} %get-tuple-element.282) | copy-start | bytes 12292
  68.0 185.2 %copy-start.68 = (f32[1024]{0:T(1024)}, f32[1024]{0:T(1024)S(1)}, u32[]{:S(2)}) copy-start(f32[1024]{0:T(1024)S(1)} %get-tuple-element.294) | copy-start | bytes 12292
  68.0 185.2 %collective-permute-start.4 = (bf16[128,1024]{1,0:T(8,128)(2,1)S(1)}, bf16[128,1024]{1,0:T(8,128)(2,1)S(1)}, u32[]{:S(2)}, u32[]{:S(2)}) collective-permute-start(bf16[128,1024]{1,0:T(8,128)(2,1)S(1)} %get-tuple-element.278), channel_id=1, source_target_pairs={{16,0},{17,1},{18,2},{19,3},{20,4},{21,5},{22,6},{23,7},{24,8},{25... | collective-permute-start | bytes 786440 | tf_op jit(solution)/shard_map/ppermute | solution.py:15
  253.4 13.9 copy-start.3
  265.7 8.6 slice-start.6
  313.3 10.1 copy-start.74
  313.3 10.1 copy-start.76
  323.4 504.9 %reduce-scatter.7.cloned.1.call-start = ((), (), s32[]{:S(2)}) async-start(), calls=%async_computation.6 | async-start | bytes 1179648 | tf_op jit(solution)/shard_map/reduce_scatter | solution.py:247
  349.6 2.6 collective-permute-start
  376.2 177.2 %copy-start.8 = (f32[4096,1024]{1,0:T(8,128)}, f32[4096,1024]{1,0:T(8,128)S(1)}, u32[]{:S(2)}) copy-start(f32[4096,1024]{1,0:T(8,128)S(1)} %get-tuple-element.300) | copy-start | bytes 50331652
  376.2 177.2 %copy-start.70 = (f32[1024]{0:T(1024)}, f32[1024]{0:T(1024)S(1)}, u32[]{:S(2)}) copy-start(f32[1024]{0:T(1024)S(1)} %get-tuple-element.280) | copy-start | bytes 12292
  376.2 177.2 %copy-start.72 = (f32[1024]{0:T(1024)}, f32[1024]{0:T(1024)S(1)}, u32[]{:S(2)}) copy-start(f32[1024]{0:T(1024)S(1)} %get-tuple-element.292) | copy-start | bytes 12292
  376.2 177.2 %collective-permute-start.3 = (bf16[128,1024]{1,0:T(8,128)(2,1)S(1)}, bf16[128,1024]{1,0:T(8,128)(2,1)S(1)}, u32[]{:S(2)}, u32[]{:S(2)}) collective-permute-start(bf16[128,1024]{1,0:T(8,128)(2,1)S(1)} %get-tuple-element.275), channel_id=1, source_target_pairs={{16,0},{17,1},{18,2},{19,3},{20,4},{21,5},{22,6},{23,7},{24,8},{25... | collective-permute-start | bytes 786440 | tf_op jit(solution)/shard_map/ppermute | solution.py:15
  553.9 13.9 copy-start.5
  566.2 8.6 slice-start.10
  602.6 8.2 copy-start.49
  623.9 206.8 %reduce-scatter.13.cloned.1.call-start = ((), (), s32[]{:S(2)}) async-start(), calls=%async_computation.9 | async-start | bytes 4456448 | tf_op jit(solution)/shard_map/reduce_scatter | solution.py:262
  634.3 310.3 %reduce-scatter.11.cloned.1.call-start = ((), (), s32[]{:S(2)}) async-start(), calls=%async_computation.8 | async-start | bytes 13369344 | tf_op jit(solution)/shard_map/reduce_scatter | solution.py:261
  657.6 635.8 %reduce-scatter.15.cloned.1.call-start = ((), (), s32[]{:S(2)}) async-start(), calls=%async_computation.10 | async-start | bytes 17825792 | tf_op jit(solution)/shard_map/reduce_scatter | solution.py:264
  686.7 961.6 %reduce-scatter.17.cloned.1.call-start = ((), (), s32[]{:S(2)}) async-start(), calls=%async_computation.11 | async-start | bytes 17825792 | tf_op jit(solution)/shard_map/reduce_scatter | solution.py:265
  736.5 90.9 %collective-permute-start.2 = (bf16[2,128,3,512]{3,1,2,0:T(8,128)(2,1)S(1)}, bf16[2,128,3,512]{3,1,2,0:T(8,128)(2,1)S(1)}, u32[]{:S(2)}, u32[]{:S(2)}) collective-permute-start(bf16[2,128,3,512]{3,1,2,0:T(8,128)(2,1)S(1)} %slice.146), channel_id=1, source_target_pairs={{16,0},{17,1},{18,2},{19,3},{20,4},{21,5},{22,6},{23,7},{24,8},{25... | collective-permute-start | bytes 2359304 | tf_op jit(solution)/shard_map/ppermute | solution.py:15
  (52 other events, 177.6 us)
Sparse Core Ops, SparseCore 0:
  323.5 10.9 reduce-scatter.8
  624.0 10.9 reduce-scatter.6
  637.8 96.2 reduce-scatter.12
  740.2 204.3 reduce-scatter.10
  947.4 345.9 reduce-scatter.14
  1296.2 352.0 reduce-scatter.16
where the time goes:
time: 1670 us; the launch traced here: 1660 us
  waiting for transfers between devices  1220 us (73%)
  matrix products  142 us (9%)
  other arithmetic  123 us (7%)
  local copies, waits for them, and re-layouts  76.3 us (5%)
  blocking collectives  45.9 us (3%)
  loops' own time  24.8 us (1%)
    ppermute x5, waiting for transfers between devices, passed_along(): return lax.ppermute(array, axis, pairs)  404 us
    reduce_scatter x1, waiting for transfers between devices, local(): lax.psum_scatter(combined[5], 'dp', scatter_dimension=0, tiled=True)  355 us
    reduce_scatter x1, waiting for transfers between devices, local(): lax.psum_scatter(combined[4], 'dp', scatter_dimension=0, tiled=True)  349 us
    reduce_scatter x1, waiting for transfers between devices, local(): lax.psum_scatter(combined[1], 'dp', scatter_dimension=0, tiled=True)  114 us
    add x6, other arithmetic, add_terms(): return tuple((left + right for left, right in zip(first, second)))  92.4 us
    unnamed x1, blocking collectives  45.9 us
    dot_general x8, matrix products, inner_left(): lax.dot_general(left, right, (((0,), (0,)), ((), ())), preferred_element_...  43.1 us
    broadcast_in_dim x8, local copies, waits for them, and re-layouts, local(): jnp.zeros(matrix.shape, jnp.float32)  37 us
  transfers between devices with their start and end apart: 11, of which 8 were waited for; matrix products, arithmetic and copies ran while one was open for 13% of the time, Pallas kernels for 0%

commit v1 on v0

v1 whole, which is shorter than its diff:
```python
import functools

import jax
import jax.numpy as jnp
from jax import lax
from jax.experimental import pallas as pl
from jax.experimental.pallas import tpu as pltpu
from jax.sharding import PartitionSpec as P

HEADS = 16
EPSILON = 1e-05
BF16 = jnp.bfloat16
F32 = jnp.float32
GROUP = 4


def dot(left, right):
    return jnp.dot(left, right, preferred_element_type=F32)


def dot_t(left, right):
    return lax.dot_general(left, right, (((1,), (1,)), ((), ())), preferred_element_type=F32)


def t_dot(left, right):
    return lax.dot_general(left, right, (((0,), (0,)), ((), ())), preferred_element_type=F32)


def head_sum(product, reduce_mat):
    high = product.astype(BF16)
    low = (product - high.astype(F32)).astype(BF16)
    return dot(high, reduce_mat) + dot(low, reduce_mat)


def head_mats(lanes, width):
    row = lax.broadcasted_iota(jnp.int32, (lanes, 128), 0)
    col = lax.broadcasted_iota(jnp.int32, (lanes, 128), 1)
    reduce_mat = (row // width == col).astype(BF16)
    row = lax.broadcasted_iota(jnp.int32, (128, lanes), 0)
    col = lax.broadcasted_iota(jnp.int32, (128, lanes), 1)
    return reduce_mat, (col // width == row).astype(BF16)


def local_probs(q, k, reduce_mat, scale):
    probs = {}
    for a in range(len(q)):
        scores = [head_sum(q[a] * k[b], reduce_mat) * scale for b in range(a + 1)]
        peak = functools.reduce(jnp.maximum, scores)
        parts = [jnp.exp(s - peak) for s in scores]
        total = functools.reduce(lambda u, v: u + v, parts)
        for b in range(a + 1):
            probs[a, b] = parts[b] / total
    return probs


def local_attn_fwd_kernel(width, q_ref, k_ref, v_ref, o_ref):
    books, _, lanes = q_ref.shape
    reduce_mat, expand_mat = head_mats(lanes, width)
    q = [q_ref[a].astype(F32) for a in range(books)]
    k = [k_ref[a].astype(F32) for a in range(books)]
    v = [v_ref[a].astype(F32) for a in range(books)]
    probs = local_probs(q, k, reduce_mat, width**-0.5)
    for a in range(books):
        mixed = [dot(probs[a, b].astype(BF16), expand_mat) * v[b] for b in range(a + 1)]
        o_ref[a] = functools.reduce(lambda s, t: s + t, mixed).astype(BF16)


def local_attn_bwd_kernel(width, q_ref, k_ref, v_ref, g_ref, dq_ref, dk_ref, dv_ref):
    books, _, lanes = q_ref.shape
    scale = width**-0.5
    reduce_mat, expand_mat = head_mats(lanes, width)
    q = [q_ref[a].astype(F32) for a in range(books)]
    k = [k_ref[a].astype(F32) for a in range(books)]
    v = [v_ref[a].astype(F32) for a in range(books)]
    g = [g_ref[a].astype(F32) for a in range(books)]
    probs = local_probs(q, k, reduce_mat, scale)
    dq = [0.0] * books
    dk = [0.0] * books
    dv = [0.0] * books
    for a in range(books):
        dprobs = [head_sum(g[a] * v[b], reduce_mat) for b in range(a + 1)]
        inner = functools.reduce(
            lambda s, t: s + t, [dprobs[b] * probs[a, b] for b in range(a + 1)]
        )
        for b in range(a + 1):
            dscore = dot((probs[a, b] * (dprobs[b] - inner)).astype(BF16), expand_mat)
            dq[a] = dq[a] + dscore * k[b]
            dk[b] = dk[b] + dscore * q[a]
            dv[b] = dv[b] + dot(probs[a, b].astype(BF16), expand_mat) * g[a]
    for a in range(books):
        dq_ref[a] = (dq[a] * scale).astype(BF16)
        dk_ref[a] = (dk[a] * scale).astype(BF16)
        dv_ref[a] = dv[a].astype(BF16)


def local_attn(packed, books, grads=None):
    micros, _, frames, wide = packed.shape
    features = wide // 3
    width = features // HEADS
    lanes = GROUP * width
    groups = features // lanes

    def spec(part):
        return pl.BlockSpec(
            (None, books, frames, lanes), lambda m, h: (m, 0, 0, part * groups + h)
        )

    own = spec(0)
    shape = jax.ShapeDtypeStruct((micros, books, frames, features), BF16)
    if grads is None:
        return pl.pallas_call(
            functools.partial(local_attn_fwd_kernel, width),
            grid=(micros, groups),
            in_specs=[spec(0), spec(1), spec(2)],
            out_specs=own,
            out_shape=shape,
            name="local_attn_fwd",
        )(packed, packed, packed)
    return pl.pallas_call(
        functools.partial(local_attn_bwd_kernel, width),
        grid=(micros, groups),
        in_specs=[spec(0), spec(1), spec(2), own],
        out_specs=[own] * 3,
        out_shape=[shape] * 3,
        name="local_attn_bwd",
    )(packed, packed, packed, grads)


def item_mask(lengths_ref, micro, frames, items):
    row = lax.broadcasted_iota(jnp.int32, (frames, frames), 0)
    col = lax.broadcasted_iota(jnp.int32, (frames, frames), 1)
    row_item = jnp.zeros((frames, frames), jnp.int32)
    col_item = jnp.zeros((frames, frames), jnp.int32)
    end = 0
    for i in range(items):
        end = end + lengths_ref[micro, 0, i]
        row_item = row_item + (row >= end).astype(jnp.int32)
        col_item = col_item + (col >= end).astype(jnp.int32)
    return (row_item == col_item) & (row >= col)


def head_parts(block, width):
    per = 128 // width
    lane = lax.broadcasted_iota(jnp.int32, (block.shape[0], 128), 1)
    parts = []
    for h in range(block.shape[1] // width):
        tile = block[:, (h // per) * 128 : (h // per + 1) * 128]
        parts.append(jnp.where(lane // width == h % per, tile, jnp.zeros_like(tile)))
    return parts


def frame_probs(q, k, mask, scale):
    scores = jnp.where(mask, dot_t(q, k) * scale, -1e30)
    parts = jnp.exp(scores - jnp.max(scores, axis=-1, keepdims=True))
    return parts / jnp.sum(parts, axis=-1, keepdims=True)


def global_attn_fwd_kernel(width, items, lengths_ref, q_ref, k_ref, v_ref, o_ref):
    frames, lanes = q_ref.shape
    mask = item_mask(lengths_ref, pl.program_id(0), frames, items)
    per = 128 // width
    q = head_parts(q_ref[...], width)
    v = head_parts(v_ref[...], width)
    mixed = [0.0] * (lanes // 128)
    for h in range(lanes // width):
        tile = slice((h // per) * 128, (h // per + 1) * 128)
        probs = frame_probs(q[h], k_ref[:, tile], mask, width**-0.5)
        mixed[h // per] = mixed[h // per] + dot(probs.astype(BF16), v[h])
    for i, tile in enumerate(mixed):
        o_ref[:, i * 128 : (i + 1) * 128] = tile.astype(BF16)


def global_attn_bwd_kernel(
    width, items, lengths_ref, q_ref, k_ref, v_ref, g_ref, dq_ref, dk_ref, dv_ref
):
    frames, lanes = q_ref.shape
    scale = width**-0.5
    mask = item_mask(lengths_ref, pl.program_id(0), frames, items)
    per = 128 // width
    q = head_parts(q_ref[...], width)
    k = head_parts(k_ref[...], width)
    g = head_parts(g_ref[...], width)
    tiles = lanes // 128
    dq, dk, dv = [0.0] * tiles, [0.0] * tiles, [0.0] * tiles
    for h in range(lanes // width):
        t = h // per
        tile = slice(t * 128, (t + 1) * 128)
        probs = frame_probs(q[h], k_ref[:, tile], mask, scale)
        dv[t] = dv[t] + t_dot(probs.astype(BF16), g[h])
        dprobs = dot_t(g[h], v_ref[:, tile])
        inner = jnp.sum(dprobs * probs, axis=-1, keepdims=True)
        dscore = (probs * (dprobs - inner)).astype(BF16)
        dq[t] = dq[t] + dot(dscore, k[h])
        dk[t] = dk[t] + t_dot(dscore, q[h])
    for t in range(tiles):
        tile = slice(t * 128, (t + 1) * 128)
        dq_ref[:, tile] = (dq[t] * scale).astype(BF16)
        dk_ref[:, tile] = (dk[t] * scale).astype(BF16)
        dv_ref[:, tile] = dv[t].astype(BF16)


def global_attn(packed, lengths, grads=None):
    micros, frames, wide = packed.shape
    features = wide // 3
    width = features // HEADS
    lanes = GROUP * width
    groups = features // lanes
    items = lengths.shape[-1]

    def spec(part):
        return pl.BlockSpec((None, frames, lanes), lambda m, h, _: (m, 0, part * groups + h))

    own = spec(0)
    shape = jax.ShapeDtypeStruct((micros, frames, features), BF16)
    operands = (lengths, packed, packed, packed)
    if grads is None:
        kernel, ins, outs, shapes = global_attn_fwd_kernel, [], own, shape
    else:
        kernel, ins, outs, shapes = global_attn_bwd_kernel, [own], [own] * 3, [shape] * 3
        operands = operands + (grads,)
    return pl.pallas_call(
        functools.partial(kernel, width, items),
        grid_spec=pltpu.PrefetchScalarGridSpec(
            num_scalar_prefetch=1,
            grid=(micros, groups),
            in_specs=[spec(0), spec(1), spec(2)] + ins,
            out_specs=outs,
        ),
        out_shape=shapes,
        name="global_attn_fwd" if grads is None else "global_attn_bwd",
    )(*operands)


def rstd(rows):
    return lax.rsqrt(jnp.mean(rows * rows, axis=-1, keepdims=True) + EPSILON)


def gelu_parts(hidden):
    c = 0.7978845608028654
    square = hidden * hidden
    t = jnp.tanh(c * hidden * (1.0 + 0.044715 * square))
    value = 0.5 * hidden * (1.0 + t)
    slope = 0.5 * (1.0 + t) + 0.5 * hidden * (1.0 - t * t) * c * (1.0 + 3 * 0.044715 * square)
    return value.astype(BF16), slope.astype(BF16)


def layer_forward(weights, rows, attend):
    gain_one, w_qkv, w_out, gain_two, w_up, w_down = weights
    normed = (rows * rstd(rows) * gain_one).astype(BF16)
    packed = dot(normed, w_qkv).astype(BF16)
    mixture = attend(packed)
    middle = rows + dot(mixture, w_out)
    normed_two = (middle * rstd(middle) * gain_two).astype(BF16)
    active, slope = gelu_parts(dot(normed_two, w_up))
    result = middle + dot(active, w_down)
    return result, (rows, normed, packed, mixture, middle, normed_two, active, slope)


def norm_backward(grad, rows, gain):
    scale = rstd(rows)
    plain = rows * scale
    grad_gain = jnp.sum(grad * plain, axis=0)
    lead = grad * gain
    return scale * (lead - plain * jnp.mean(lead * plain, axis=-1, keepdims=True)), grad_gain


def layer_backward(weights, stored, low_out, grad_out, attend_back, reduce):
    gain_one, w_qkv, w_out, gain_two, w_up, w_down = weights
    rows, normed, packed, mixture, middle, normed_two, active, slope = stored
    grad_down = reduce(active, low_out)
    grad_hidden = (slope.astype(F32) * dot_t(low_out, w_down)).astype(BF16)
    grad_up = reduce(normed_two, grad_hidden)
    grad_middle, grad_gain_two = norm_backward(dot_t(grad_hidden, w_up), middle, gain_two)
    grad_middle = grad_middle + grad_out
    low_middle = grad_middle.astype(BF16)
    grad_wout = reduce(mixture, low_middle)
    grad_packed = attend_back(packed, dot_t(low_middle, w_out).astype(BF16))
    grad_qkv = reduce(normed, grad_packed)
    grad_in, grad_gain_one = norm_backward(dot_t(grad_packed, w_qkv), rows, gain_one)
    grads = (grad_gain_one, grad_qkv, grad_wout, grad_gain_two, grad_up, grad_down)
    return grad_in + grad_middle, grads


def swap(size, by):
    return [(i, i ^ by) for i in range(size)]


class Reducer:
    def __init__(self, core, size, spots):
        self.core, self.size = core, size
        self.index = lax.axis_index("dp")
        self.spots = spots
        self.depth = size // 4

    def permute(self, array, pairs):
        base = self.core * self.size
        return lax.ppermute(array, ("section", "dp"), [(base + i, base + j) for i, j in pairs])

    def quarters(self, left):
        rows, columns = left.shape
        block = columns // self.size
        if block % 128 == 0:
            split = left.reshape(rows, self.depth, 2, 2, block)
            x, y = self.index % 2, (self.index // 2) % 2
            out = {}
            for dy in range(2):
                for dx in range(2):
                    one = lax.dynamic_index_in_dim(split, y ^ dy, 2, keepdims=False)
                    one = lax.dynamic_index_in_dim(one, x ^ dx, 2, keepdims=False)
                    out[dx, dy] = one.reshape(rows, self.depth * block)
            return out
        placed = dot(left, self.spots(columns)).astype(BF16)
        wide = self.depth * block
        return {
            (dx, dy): placed[:, (2 * dy + dx) * wide : (2 * dy + dx + 1) * wide]
            for dy in range(2)
            for dx in range(2)
        }

    def half(self, left, right, by_first, by_second, far, near):
        first = self.permute(t_dot(left[1, 1], right).astype(BF16), swap(self.size, by_first))
        second = self.permute(t_dot(left[near], right).astype(BF16), swap(self.size, by_first))
        onward = (t_dot(left[far], right) + first.astype(F32)).astype(BF16)
        onward = self.permute(onward, swap(self.size, by_second))
        return (t_dot(left[0, 0], right) + second.astype(F32) + onward.astype(F32)).astype(BF16)

    def along_z(self, total):
        if self.depth != 4:
            groups = [[4 * z + place for z in range(self.depth)] for place in range(4)]
            return lax.psum_scatter(
                total, "dp", scatter_dimension=0, axis_index_groups=groups, tiled=True
            )[0].astype(F32)
        z = self.index // 4

        def piece(at):
            return lax.dynamic_index_in_dim(
                total, jnp.clip(at, 0, self.depth - 1), 0, keepdims=False
            )

        up = down = None
        for step in range(1, self.depth):
            send_up = piece(self.depth - step + z)
            send_down = piece(z - self.depth + step)
            if up is not None:
                send_up = (send_up.astype(F32) + up.astype(F32)).astype(BF16)
                send_down = (send_down.astype(F32) + down.astype(F32)).astype(BF16)
            pairs = [(4 * k + i, 4 * k + 4 + i) for k in range(step) for i in range(4)]
            up = self.permute(send_up, pairs)
            last = self.size - 1
            down = self.permute(send_down, [(last - i, last - j) for i, j in pairs])
        return piece(z).astype(F32) + up.astype(F32) + down.astype(F32)

    def __call__(self, left, right):
        parts = right.shape[1] // 2
        quarters = self.quarters(left)
        total = jnp.concatenate(
            [
                self.half(quarters, right[:, :parts], 1, 2, (0, 1), (1, 0)),
                self.half(quarters, right[:, parts:], 2, 1, (1, 0), (0, 1)),
            ],
            axis=1,
        )
        return self.along_z(total.reshape(self.depth, -1, right.shape[1]))


def spots_of(size):
    index = lax.axis_index("dp")
    kept = {}

    def spots(columns):
        if columns not in kept:
            block, depth = columns // size, size // 4
            source = lax.broadcasted_iota(jnp.int32, (columns, columns), 0)
            target = lax.broadcasted_iota(jnp.int32, (columns, columns), 1)
            place = target // (depth * block)
            z = (target // block) % depth
            at = (z * 4 + (place ^ (index % 4))) * block + target % block
            kept[columns] = (source == at).astype(BF16)
        return kept[columns]

    return spots


def sum_over_dp(array, size):
    if size & (size - 1):
        return lax.psum(array, "dp")
    by = 1
    while by < size:
        array = array + lax.ppermute(array, "dp", swap(size, by))
        by *= 2
    return array


def local(codebook_embed, item_lengths, gain_attn, w_qkv, w_out, gain_mlp, w_up, w_down, cotangent):
    section = lax.axis_index("section")
    size = lax.axis_size("dp")
    first_core = section == 0
    weights = (gain_attn[0], w_qkv[0], w_out[0], gain_mlp[0], w_up[0], w_down[0])
    micros, frames, books, features = codebook_embed.shape
    scale_in = books**-0.5
    half_width = features // 2
    spots = spots_of(size)

    embed = codebook_embed.transpose(0, 2, 1, 3).astype(F32)
    upstream = cotangent.transpose(0, 2, 1, 3).reshape(-1, features)

    frame_in = (jnp.sum(embed, axis=1) * scale_in).reshape(-1, features)
    frame_out, frame_kept = layer_forward(
        weights,
        frame_in,
        lambda packed: global_attn(
            packed.reshape(micros, frames, -1), item_lengths
        ).reshape(-1, features),
    )
    states = lax.ppermute(frame_out.astype(BF16), "section", [(0, 1)])
    states = states.astype(F32).reshape(micros, 1, frames, features)
    local_in = (embed + states).reshape(-1, features)
    local_out, local_kept = layer_forward(
        weights,
        local_in,
        lambda packed: local_attn(
            packed.reshape(micros, books, frames, -1), books
        ).reshape(-1, features),
    )
    local_out = local_out.astype(BF16)
    other_half = lax.ppermute(local_out[:, :half_width], "section", [(1, 0)])
    own_half = jnp.where(first_core, other_half, local_out[:, half_width:])

    def local_back(packed, grads):
        parts = local_attn(
            packed.reshape(micros, books, frames, -1),
            books,
            grads.reshape(micros, books, frames, -1),
        )
        return jnp.concatenate(parts, axis=-1).reshape(-1, 3 * features)

    def global_back(packed, grads):
        parts = global_attn(
            packed.reshape(micros, frames, -1), item_lengths, grads.reshape(micros, frames, -1)
        )
        return jnp.concatenate(parts, axis=-1).reshape(-1, 3 * features)

    local_grad, local_terms = layer_backward(
        weights, local_kept, upstream, upstream.astype(F32), local_back, Reducer(1, size, spots)
    )
    local_grad = local_grad.reshape(micros, books, frames, features)
    frame_grad = jnp.sum(local_grad, axis=1).astype(BF16).reshape(-1, features)
    frame_grad = lax.ppermute(frame_grad, "section", [(1, 0)])
    global_grad, global_terms = layer_backward(
        weights, frame_kept, frame_grad, frame_grad.astype(F32), global_back, Reducer(0, size, spots)
    )
    global_grad = (global_grad * scale_in).reshape(micros, 1, frames, features)

    sent_local = lax.ppermute(local_grad[..., :half_width].astype(BF16), "section", [(1, 0)])
    sent_global = lax.ppermute(global_grad[..., half_width:].astype(BF16), "section", [(0, 1)])
    embed_grad = jnp.where(
        first_core, sent_local.astype(F32), local_grad[..., half_width:]
    ) + jnp.where(first_core, global_grad[..., :half_width], sent_global.astype(F32))

    terms = [jnp.where(first_core, g, l) for g, l in zip(global_terms, local_terms)]
    gains = sum_over_dp(jnp.stack([terms[0], terms[3]]), size).reshape(2, size, -1)
    gains = lax.dynamic_index_in_dim(gains, lax.axis_index("dp"), 1, keepdims=False)

    def placed(rows):
        return rows.reshape(micros, books, frames, -1).transpose(0, 2, 1, 3)

    return (
        placed(own_half),
        placed(embed_grad),
        gains[:1],
        terms[1][None],
        terms[2][None],
        gains[1:],
        terms[4][None],
        terms[5][None],
    )


def solution(mesh):
    in_specs = (
        P(None, "dp", None, None),
        P(None, "dp", None),
        P("section", None),
        P("section", None, None),
        P("section", None, None),
        P("section", None),
        P("section", None, None),
        P("section", None, None),
        P(None, "dp", None, None),
    )
    out_specs = (
        P(None, "dp", None, "section"),
        P(None, "dp", None, "section"),
        P("section", "dp"),
        P("section", "dp", None),
        P("section", "dp", None),
        P("section", "dp"),
        P("section", "dp", None),
        P("section", "dp", None),
    )
    return jax.shard_map(local, mesh=mesh, in_specs=in_specs, out_specs=out_specs, check_vma=False)
```

time: 1670 us -> 869 us (0.52)
  waiting for transfers between devices: 1220 us -> 105 us
  starting transfers between devices: 6.71 us -> 238 us
  local copies, waits for them, and re-layouts: 76.3 us -> 171 us
  matrix products: 142 us -> 230 us
  other arithmetic: 123 us -> 65.8 us
  blocking collectives: 45.9 us -> 0 us
  Pallas kernels: 0 us -> 42.9 us
  loops' own time: 24.8 us -> 0 us
    reduce_scatter x6 -> x0, waiting for transfers between devices: 818 us -> none  [the longest x1 355 us: local(): lax.psum_scatter(combined[5], 'dp', scatter_dimension=0, tiled=True)]
    ppermute x5 -> x105, waiting for transfers between devices: 404 us -> 105 us  [the longest x96 101 us: permute(): lax.ppermute(array, ('section', 'dp'), [(base + i, base + j) for i, j in...]
    ppermute x5 -> x105, starting transfers between devices: 6.46 us -> 238 us  [the longest x96 200 us: permute(): lax.ppermute(array, ('section', 'dp'), [(base + i, base + j) for i, j in...]
    add x10 -> x6, other arithmetic: 92.8 us -> 1.26 us  [the longest x1 1.15 us: local(): local_in = (embed + states).reshape(-1, features)]
    dot_general x44 -> x86, matrix products: 139 us -> 230 us  [the longest x64 102 us: t_dot(): lax.dot_general(left, right, (((0,), (0,)), ((), ())), preferred_element_...]
    unnamed x68 -> x300, local copies, waits for them, and re-layouts: 13.2 us -> 81.5 us
    dynamic_slice x0 -> x7, local copies, waits for them, and re-layouts: none -> 53.6 us  [the longest x5 30.5 us: piece(): lax.dynamic_index_in_dim(total, jnp.clip(at, 0, self.depth - 1), 0, keepd...]
    unnamed x1 -> x0, blocking collectives: 45.9 us -> none
  transfers between devices with their start and end apart: 11 -> 105, of which waited for: 8 -> 19; matrix products, arithmetic and copies ran while one was open for 13% -> 30% of each run, Pallas kernels for 0% -> 2%
where the time goes in v1:
time: 869 us; the launch traced here: 857 us
  starting transfers between devices  238 us (27%)
  matrix products  230 us (26%)
  local copies, waits for them, and re-layouts  171 us (20%)
  waiting for transfers between devices  105 us (12%)
  other arithmetic  65.8 us (8%)
  Pallas kernels  42.9 us (5%)
    ppermute x96, starting transfers between devices, permute(): lax.ppermute(array, ('section', 'dp'), [(base + i, base + j) for i, j in...  200 us
    dot_general x64, matrix products, t_dot(): lax.dot_general(left, right, (((0,), (0,)), ((), ())), preferred_element_...  102 us
    ppermute x96, waiting for transfers between devices, permute(): lax.ppermute(array, ('section', 'dp'), [(base + i, base + j) for i, j in...  101 us
    unnamed x300, local copies, waits for them, and re-layouts  81.5 us
    dot_general x14, matrix products, dot(): return jnp.dot(left, right, preferred_element_type=F32)  68.4 us
    dot_general x8, matrix products, dot_t(): lax.dot_general(left, right, (((1,), (1,)), ((), ())), preferred_element_...  60 us
    dynamic_slice x5, local copies, waits for them, and re-layouts, piece(): lax.dynamic_index_in_dim(total, jnp.clip(at, 0, self.depth - 1), 0, keepd...  30.5 us
    dynamic_slice x2, local copies, waits for them, and re-layouts, quarters(): one = lax.dynamic_index_in_dim(one, x ^ dx, 2, keepdims=False)  23.1 us
  transfers between devices with their start and end apart: 105, of which 19 were waited for; matrix products, arithmetic and copies ran while one was open for 30% of the time, Pallas kernels for 2%

profile of v1, /device:TPU:0, one launch (start us, length us, event | category | flops | bytes accessed | tf_op | source)
XLA Modules:
  0.0 857.5 jit_solution(14031985690694944195)
XLA Ops:
  7.8 9.4 %global_attn_fwd.1 = bf16[2,128,1024]{2,1,0:T(8,128)(2,1)} custom-call(s32[2,1,8]{2,1,0:T(1,128)} %lengths_ref.3, bf16[2,128,3072]{2,1,0:T(8,128)(2,1)} %bitcast.362, bf16[2,128,3072]{2,1,0:T(8,128)(2,1)} %bitcast.363, bf16[2,128,3072]{2,1,0:T(8,128)(2,1)} %bitcast.364), custom_call_target="tpu_custom_call" | custom-call | tf_op jit(solution)/shard_map/global_attn_fwd/pallas_call | solution.py:221
  19.6 9.0 %multiply_convert_fusion.2 = (bf16[256,4096]{1,0:T(8,128)(2,1)S(1)}, f32[256,4096]{1,0:T(8,128)}) fusion(bf16[1,1024,4096]{2,1,0:T(8,128)(2,1)} %param.15, f32[256,1024]{1,0:T(8,128)S(1)} %get-tuple-element.84, f32[1024]{0:T(1024)S(1)} %bitcast.462, f32[256]{0:T(256)S(1)} %add_rsqrt_fusion.2), kind=kOutput, calls=%fused_computation.44 | convolution fusion | flops 2157707264 | bytes 15733760 | tf_op jit(solution)/shard_map/dot_general | solution.py:18
  70.5 9.0 %fusion.32 = bf16[768,3072]{1,0:T(8,128)(2,1)} fusion(bf16[768,1024]{1,0:T(8,128)(2,1)} %bitcast.446, bf16[1,1024,3072]{2,1,0:T(8,128)(2,1)} %param.12), kind=kOutput, calls=%fused_computation.35 | convolution fusion | flops 4834197504 | bytes 12582912 | tf_op jit(solution)/shard_map/dot_general | solution.py:18
  79.5 8.4 local_attn_fwd.1
  92.1 17.2 %multiply_convert_fusion.1 = (bf16[768,4096]{1,0:T(8,128)(2,1)}, f32[768,4096]{1,0:T(8,128)}) fusion(bf16[1,1024,4096]{2,1,0:T(8,128)(2,1)} %param.15, f32[768,1024]{1,0:T(8,128)S(1)} %get-tuple-element.88, f32[1024]{0:T(1024)S(1)} %bitcast.464, f32[768]{0:T(1024)S(1)} %add_rsqrt_fusion), kind=kOutput, calls=%fused_computation.2 | convolution fusion | flops 6473121792 | bytes 30415872 | tf_op jit(solution)/shard_map/dot_general | solution.py:18
  109.3 18.3 %multiply_convert_fusion = bf16[768,4096]{1,0:T(8,128)(2,1)} fusion(bf16[768,1024]{1,0:T(8,128)(2,1)S(1)} %bitcast.412, bf16[1,4096,1024]{2,1,0:T(8,128)(2,1)} %param.16, f32[768,4096]{1,0:T(8,128)} %get-tuple-element.90), kind=kOutput, calls=%fused_computation | convolution fusion | flops 6505365504 | bytes 28835840 | tf_op jit(solution)/shard_map/dot_general | solution.py:22
  127.7 12.2 %multiply_reduce_fusion = (f32[1024]{0:T(1024)}, f32[768]{0:T(1024)S(1)}, f32[768,1024]{1,0:T(8,128)S(1)}) fusion(f32[768,1024]{1,0:T(8,128)S(1)} %get-tuple-element.88, f32[768]{0:T(1024)S(1)} %add_rsqrt_fusion, f32[1024]{0:T(1024)S(1)} %bitcast.465, bf16[768,4096]{1,0:T(8,128)(2,1)} %multiply_convert_fusion, bf16[1,1024,4096]{2,1,0:T(8,128)(2,1)} %param.15), kind=kOutput, calls=%fused_computation.52 | convolution fusion | flops 6447167488 | bytes 20985856 | tf_op jit(solution)/shard_map/dot_general | solution.py:22
  144.6 12.1 %local_attn_bwd.1 = (bf16[2,3,128,1024]{3,2,1,0:T(8,128)(2,1)}, bf16[2,3,128,1024]{3,2,1,0:T(8,128)(2,1)}, bf16[2,3,128,1024]{3,2,1,0:T(8,128)(2,1)}) custom-call(bf16[2,3,128,3072]{3,2,1,0:T(8,128)(2,1)} %bitcast.359, bf16[2,3,128,3072]{3,2,1,0:T(8,128)(2,1)} %bitcast.360, bf16[2,3,128,3072]{3,2,1,0:T(8,128)(2,1)} %bitcast.361, ...), custom_call_target="tpu_custom_call" | custom-call | tf_op jit(solution)/shard_map/local_attn_bwd/pallas_call | solution.py:119
  160.0 8.9 %multiply_reduce_fusion.1 = (f32[1024]{0:T(1024)S(1)}, f32[768]{0:T(1024)S(1)}, f32[768,1024]{1,0:T(8,128)S(1)}) fusion(f32[2,3,128,1024]{3,2,1,0:T(8,128)S(1)} %copy-done.26, f32[768]{0:T(1024)S(1)} %rsqrt.48, f32[1024]{0:T(1024)S(1)} %bitcast.480, bf16[768,3072]{1,0:T(8,128)(2,1)S(1)} %bitcast.380, bf16[1,1024,3072]{2,1,0:T(8,128)(2,1)} %param.12), kind=kOutput, calls=%fused_computation.53 | convolution fusion | flops 4836554752 | bytes 17315840 | tf_op jit(solution)/shard_map/dot_general | solution.py:22
  214.7 11.1 %reshape.406 = bf16[768,4,2,2,256]{4,3,2,1,0:T(2,128)(2,1)} reshape(bf16[768,4096]{1,0:T(8,128)(2,1)} %get-tuple-element.89) | data formatting | bytes 12582912 | tf_op jit(solution)/shard_map/reshape | solution.py:303
  225.8 16.1 %constant_dynamic-slice_fusion.7 = (bf16[768,4,1,1,256]{4,3,2,1,0:T(2,128)(2,1)}, bf16[768,4,1,1,256]{4,3,2,1,0:T(2,128)(2,1)}, bf16[768,4,1,1,256]{4,3,2,1,0:T(2,128)(2,1)}, bf16[768,4,1,1,256]{4,3,2,1,0:T(2,128)(2,1)}) fusion(bf16[768,4,2,2,256]{4,3,2,1,0:T(2,128)(2,1)} %reshape.406, s32[]{:T(128)S(6)} %select_n.275, s32[]{:T(128)S(6)} %select_n.271, ...), kind=kLoop, calls=%fused_computation.427 | loop fusion | bytes 12582928 | tf_op jit(solution)/shard_map/jit(dynamic_index_in_dim)/dynamic_slice | solution.py:309
  255.9 8.2 copy.98
  325.4 13.1 %global_attn_bwd.1 = (bf16[2,128,1024]{2,1,0:T(8,128)(2,1)}, bf16[2,128,1024]{2,1,0:T(8,128)(2,1)}, bf16[2,128,1024]{2,1,0:T(8,128)(2,1)}) custom-call(s32[2,1,8]{2,1,0:T(1,128)} %lengths_ref.3, bf16[2,128,3072]{2,1,0:T(8,128)(2,1)} %bitcast.365, bf16[2,128,3072]{2,1,0:T(8,128)(2,1)} %bitcast.366, bf16[2,128,3072]{2,1,0:T(8,128)(2,1)} %bitcast.367, ...), custom_call_target="tpu_custom_call" | custom-call | tf_op jit(solution)/shard_map/global_attn_bwd/pallas_call | solution.py:221
  393.3 15.8 %collective-permute-start.8 = (f32[2,1024]{1,0:T(2,128)S(1)}, f32[2,1024]{1,0:T(2,128)S(1)}, u32[]{:S(2)}, u32[]{:S(2)}) collective-permute-start(f32[2,1024]{1,0:T(2,128)S(1)} %add.676), channel_id=1, source_target_pairs={{0,8},{1,9},{2,10},{3,11},{4,12},{5,13},{6,14},{7,15},{8,0},{9,1},... | collective-permute-start | bytes 24584 | tf_op jit(solution)/shard_map/ppermute | solution.py:389
  419.6 9.5 %collective-permute-start.4 = (bf16[2,1,128,512]{3,2,0,1:T(8,128)(2,1)}, bf16[2,1,128,512]{3,2,0,1:T(8,128)(2,1)S(1)}, u32[]{:S(2)}, u32[]{:S(2)}) collective-permute-start(bf16[2,1,128,512]{3,2,0,1:T(8,128)(2,1)} %slice.508), channel_id=1, source_target_pairs={{0,16},{1,17},{2,18},{3,19},{4,20},{5,21},{6,22},{7,23},{8,24},{9,... | collective-permute-start | bytes 786440 | tf_op jit(solution)/shard_map/ppermute | solution.py:455
  510.3 12.4 %collective-permute-done.85 = bf16[1024,512]{0,1:T(8,128)(2,1)S(1)} collective-permute-done((bf16[1024,512]{0,1:T(8,128)(2,1)S(1)}, bf16[1024,512]{0,1:T(8,128)(2,1)S(1)}, u32[]{:S(2)}, u32[]{:S(2)}) %collective-permute-start.85) | collective-permute-done | bytes 1048608 | tf_op jit(solution)/shard_map/ppermute | solution.py:297
  551.6 8.9 %collective-permute-done.12 = bf16[256,1536]{1,0:T(8,128)(2,1)S(1)} collective-permute-done((bf16[256,1536]{1,0:T(8,128)(2,1)S(1)}, bf16[256,1536]{1,0:T(8,128)(2,1)S(1)}, u32[]{:S(2)}, u32[]{:S(2)}) %collective-permute-start.12) | collective-permute-done | bytes 786464 | tf_op jit(solution)/shard_map/ppermute | solution.py:297
  561.3 15.5 %collective-permute-done.14 = bf16[256,1536]{1,0:T(8,128)(2,1)S(1)} collective-permute-done((bf16[256,1536]{1,0:T(8,128)(2,1)S(1)}, bf16[256,1536]{1,0:T(8,128)(2,1)S(1)}, u32[]{:S(2)}, u32[]{:S(2)}) %collective-permute-start.14) | collective-permute-done | bytes 786464 | tf_op jit(solution)/shard_map/ppermute | solution.py:297
  639.0 8.4 collective-permute-done.83
  662.8 16.5 %constant_dynamic-slice_fusion.5 = (bf16[1,256,1024]{1,0,2:T(2,128)(2,1)}, bf16[1,256,1024]{1,0,2:T(2,128)(2,1)}, bf16[1,256,1024]{1,0,2:T(2,128)(2,1)}, bf16[1,...) fusion(bf16[4,256,1024]{1,0,2:T(4,128)(2,1)S(1)} %copy-done.1, ...), kind=kLoop, calls=%fused_computation.425 | loop fusion | bytes 14680092 | tf_op jit(solution)/shard_map/jit(dynamic_index_in_dim)/dynamic_slice | solution.py:336
  776.9 10.8 %collective-permute-done.64 = bf16[64,4096]{1,0:T(8,128)(2,1)S(1)} collective-permute-done((bf16[64,4096]{1,0:T(8,128)(2,1)S(1)}, bf16[64,4096]{1,0:T(8,128)(2,1)S(1)}, u32[]{:S(2)}, u32[]{:S(2)}) %collective-permute-start.64) | collective-permute-done | bytes 524320 | tf_op jit(solution)/shard_map/ppermute | solution.py:297
  796.0 9.6 %collective-permute-done.88 = bf16[256,1024]{1,0:T(8,128)(2,1)S(1)} collective-permute-done((bf16[256,1024]{1,0:T(8,128)(2,1)S(1)}, bf16[256,1024]{1,0:T(8,128)(2,1)S(1)}, u32[]{:S(2)}, u32[]{:S(2)}) %collective-permute-start.88) | collective-permute-done | bytes 524320 | tf_op jit(solution)/shard_map/ppermute | solution.py:297
  816.2 18.4 %collective-permute-start.65 = (bf16[64,4096]{1,0:T(8,128)(2,1)S(1)}, bf16[64,4096]{1,0:T(8,128)(2,1)S(1)}, u32[]{:S(2)}, u32[]{:S(2)}) collective-permute-start(bf16[64,4096]{1,0:T(8,128)(2,1)S(1)} %get-tuple-element.54), channel_id=1, source_target_pairs={{0,4},{1,5},{2,6},{3,7},{4,8},{5,9},{6,10},{7,11},{8,12},{9,13},{1... | collective-permute-start | bytes 1572872 | tf_op jit(solution)/shard_map/ppermute | solution.py:297
  845.4 8.9 %collective-permute-done.89 = bf16[256,1024]{1,0:T(8,128)(2,1)S(1)} collective-permute-done((bf16[256,1024]{1,0:T(8,128)(2,1)S(1)}, bf16[256,1024]{1,0:T(8,128)(2,1)S(1)}, u32[]{:S(2)}, u32[]{:S(2)}) %collective-permute-start.89) | collective-permute-done | bytes 524320 | tf_op jit(solution)/shard_map/ppermute | solution.py:297
  (693 shorter events, 565.5 us)
Async XLA Ops:
  271.7 170.0 %collective-permute-start.1 = (bf16[768,512]{1,0:T(8,128)(2,1)}, bf16[768,512]{1,0:T(8,128)(2,1)}, u32[]{:S(2)}, u32[]{:S(2)}) collective-permute-start(bf16[768,512]{1,0:T(8,128)(2,1)} %slice.202), channel_id=1, source_target_pairs={{16,0},{17,1},{18,2},{19,3},{20,4},{21,5},{22,6},{23,7},{24,8},{25... | collective-permute-start | bytes 2359304 | tf_op jit(solution)/shard_map/ppermute | solution.py:426
  277.9 86.9 %collective-permute-start.48 = (bf16[256,512]{1,0:T(8,128)(2,1)}, bf16[256,512]{1,0:T(8,128)(2,1)S(1)}, u32[]{:S(2)}, u32[]{:S(2)}) collective-permute-start(bf16[256,512]{1,0:T(8,128)(2,1)} %convolution_convert_fusion.31), channel_id=1, source_target_pairs={{16,18},{17,19},{18,16},{19,17},{20,22},{21,23},{22,20},{23,21},{2... | collective-permute-start | bytes 786440 | tf_op jit(solution)/shard_map/ppermute | solution.py:297
  305.4 64.3 %collective-permute-start.45 = (bf16[256,512]{1,0:T(8,128)(2,1)}, bf16[256,512]{1,0:T(8,128)(2,1)}, u32[]{:S(2)}, u32[]{:S(2)}) collective-permute-start(bf16[256,512]{1,0:T(8,128)(2,1)} %convolution_convert_fusion.33), channel_id=1, source_target_pairs={{16,17},{17,16},{18,19},{19,18},{20,21},{21,20},{22,23},{23,22},{2... | collective-permute-start | bytes 786440 | tf_op jit(solution)/shard_map/ppermute | solution.py:297
  309.0 57.4 %collective-permute-start.50 = (bf16[256,512]{1,0:T(8,128)(2,1)}, bf16[256,512]{1,0:T(8,128)(2,1)}, u32[]{:S(2)}, u32[]{:S(2)}) collective-permute-start(bf16[256,512]{1,0:T(8,128)(2,1)} %add_convert_fusion.28), channel_id=1, source_target_pairs={{16,17},{17,16},{18,19},{19,18},{20,21},{21,20},{22,23},{23,22},{2... | collective-permute-start | bytes 786440 | tf_op jit(solution)/shard_map/ppermute | solution.py:297
  311.5 58.3 %collective-permute-start.47 = (bf16[256,512]{1,0:T(8,128)(2,1)}, bf16[256,512]{1,0:T(8,128)(2,1)}, u32[]{:S(2)}, u32[]{:S(2)}) collective-permute-start(bf16[256,512]{1,0:T(8,128)(2,1)} %add_convert_fusion.30), channel_id=1, source_target_pairs={{16,18},{17,19},{18,16},{19,17},{20,22},{21,23},{22,20},{23,21},{2... | collective-permute-start | bytes 786440 | tf_op jit(solution)/shard_map/ppermute | solution.py:297
  364.8 54.8 %collective-permute-start.25 = (bf16[256,1536]{1,0:T(8,128)(2,1)}, bf16[256,1536]{1,0:T(8,128)(2,1)}, u32[]{:S(2)}, u32[]{:S(2)}) collective-permute-start(bf16[256,1536]{1,0:T(8,128)(2,1)} %convolution_convert_fusion), channel_id=1, source_target_pairs={{16,18},{17,19},{18,16},{19,17},{20,22},{21,23},{22,20},{23,21},{2... | collective-permute-start | bytes 2359304 | tf_op jit(solution)/shard_map/ppermute | solution.py:297
  372.5 44.3 %collective-permute-start.54 = (bf16[64,1024]{1,0:T(8,128)(2,1)}, bf16[64,1024]{1,0:T(8,128)(2,1)}, u32[]{:S(2)}, u32[]{:S(2)}) collective-permute-start(bf16[64,1024]{1,0:T(8,128)(2,1)} %get-tuple-element.78), channel_id=1, source_target_pairs={{31,27},{30,26},{29,25},{28,24}} | collective-permute-start | bytes 393224 | tf_op jit(solution)/shard_map/ppermute | solution.py:297
  432.9 41.9 %collective-permute-start.97 = (bf16[1024,512]{0,1:T(8,128)(2,1)S(1)}, bf16[1024,512]{0,1:T(8,128)(2,1)S(1)}, u32[]{:S(2)}, u32[]{:S(2)}) collective-permute-start(bf16[1024,512]{0,1:T(8,128)(2,1)S(1)} %copy-done.122), channel_id=1, source_target_pairs={{16,18},{17,19},{18,16},{19,17},{20,22},{21,23},{22,20},{23,21},{2... | collective-permute-start | bytes 3145736 | tf_op jit(solution)/shard_map/ppermute | solution.py:297
  493.7 38.2 %collective-permute-start.58 = (bf16[256,2048]{1,0:T(8,128)(2,1)S(1)}, bf16[256,2048]{1,0:T(8,128)(2,1)S(1)}, u32[]{:S(2)}, u32[]{:S(2)}) collective-permute-start(bf16[256,2048]{1,0:T(8,128)(2,1)S(1)} %copy-done.92), channel_id=1, source_target_pairs={{0,1},{1,0},{2,3},{3,2},{4,5},{5,4},{6,7},{7,6},{8,9},{9,8},{10,11... | collective-permute-start | bytes 3145736 | tf_op jit(solution)/shard_map/ppermute | solution.py:297
  537.3 42.4 %collective-permute-start.72 = (bf16[256,2048]{1,0:T(8,128)(2,1)S(1)}, bf16[256,2048]{1,0:T(8,128)(2,1)S(1)}, u32[]{:S(2)}, u32[]{:S(2)}) collective-permute-start(bf16[256,2048]{1,0:T(8,128)(2,1)S(1)} %copy-done.119), channel_id=1, source_target_pairs={{16,18},{17,19},{18,16},{19,17},{20,22},{21,23},{22,20},{23,21},{2... | collective-permute-start | bytes 3145736 | tf_op jit(solution)/shard_map/ppermute | solution.py:297
  583.2 73.5 %collective-permute-start.60 = (bf16[256,2048]{1,0:T(8,128)(2,1)}, bf16[256,2048]{1,0:T(8,128)(2,1)}, u32[]{:S(2)}, u32[]{:S(2)}) collective-permute-start(bf16[256,2048]{1,0:T(8,128)(2,1)} %convolution_convert_fusion.9), channel_id=1, source_target_pairs={{0,2},{1,3},{2,0},{3,1},{4,6},{5,7},{6,4},{7,5},{8,10},{9,11},{10,... | collective-permute-start | bytes 3145736 | tf_op jit(solution)/shard_map/ppermute | solution.py:297
  589.8 45.8 %collective-permute-start.81 = (bf16[1024,512]{0,1:T(8,128)(2,1)}, bf16[1024,512]{0,1:T(8,128)(2,1)}, u32[]{:S(2)}, u32[]{:S(2)}) collective-permute-start(bf16[1024,512]{0,1:T(8,128)(2,1)} %convolution_convert_fusion.26), channel_id=1, source_target_pairs={{0,1},{1,0},{2,3},{3,2},{4,5},{5,4},{6,7},{7,6},{8,9},{9,8},{10,11... | collective-permute-start | bytes 3145736 | tf_op jit(solution)/shard_map/ppermute | solution.py:297
  619.9 38.3 %collective-permute-start.62 = (bf16[256,2048]{1,0:T(8,128)(2,1)S(1)}, bf16[256,2048]{1,0:T(8,128)(2,1)}, u32[]{:S(2)}, u32[]{:S(2)}) collective-permute-start(bf16[256,2048]{1,0:T(8,128)(2,1)S(1)} %add_convert_fusion.16), channel_id=1, source_target_pairs={{0,1},{1,0},{2,3},{3,2},{4,5},{5,4},{6,7},{7,6},{8,9},{9,8},{10,11... | collective-permute-start | bytes 3145736 | tf_op jit(solution)/shard_map/ppermute | solution.py:297
  630.4 48.9 %collective-permute-start.57 = (bf16[256,2048]{1,0:T(8,128)(2,1)}, bf16[256,2048]{1,0:T(8,128)(2,1)}, u32[]{:S(2)}, u32[]{:S(2)}) collective-permute-start(bf16[256,2048]{1,0:T(8,128)(2,1)} %convolution_convert_fusion.11), channel_id=1, source_target_pairs={{0,1},{1,0},{2,3},{3,2},{4,5},{5,4},{6,7},{7,6},{8,9},{9,8},{10,11... | collective-permute-start | bytes 3145736 | tf_op jit(solution)/shard_map/ppermute | solution.py:297
  635.6 45.1 %collective-permute-start.59 = (bf16[256,2048]{1,0:T(8,128)(2,1)}, bf16[256,2048]{1,0:T(8,128)(2,1)}, u32[]{:S(2)}, u32[]{:S(2)}) collective-permute-start(bf16[256,2048]{1,0:T(8,128)(2,1)} %add_convert_fusion.18), channel_id=1, source_target_pairs={{0,2},{1,3},{2,0},{3,1},{4,6},{5,7},{6,4},{7,5},{8,10},{9,11},{10,... | collective-permute-start | bytes 3145736 | tf_op jit(solution)/shard_map/ppermute | solution.py:297
  647.4 94.1 %collective-permute-start.18 = (bf16[64,3072]{1,0:T(8,128)(2,1)}, bf16[64,3072]{1,0:T(8,128)(2,1)}, u32[]{:S(2)}, u32[]{:S(2)}) collective-permute-start(bf16[64,3072]{1,0:T(8,128)(2,1)} %get-tuple-element.65), channel_id=1, source_target_pairs={{15,11},{14,10},{13,9},{12,8}} | collective-permute-start | bytes 1179656 | tf_op jit(solution)/shard_map/ppermute | solution.py:297
  656.7 78.4 %collective-permute-start.75 = (bf16[64,4096]{1,0:T(8,128)(2,1)}, bf16[64,4096]{1,0:T(8,128)(2,1)}, u32[]{:S(2)}, u32[]{:S(2)}) collective-permute-start(bf16[64,4096]{1,0:T(8,128)(2,1)} %get-tuple-element.60), channel_id=1, source_target_pairs={{16,20},{17,21},{18,22},{19,23}} | collective-permute-start | bytes 1572872 | tf_op jit(solution)/shard_map/ppermute | solution.py:297
  658.3 103.6 %collective-permute-start.78 = (bf16[64,4096]{1,0:T(8,128)(2,1)}, bf16[64,4096]{1,0:T(8,128)(2,1)}, u32[]{:S(2)}, u32[]{:S(2)}) collective-permute-start(bf16[64,4096]{1,0:T(8,128)(2,1)} %get-tuple-element.61), channel_id=1, source_target_pairs={{31,27},{30,26},{29,25},{28,24}} | collective-permute-start | bytes 1572872 | tf_op jit(solution)/shard_map/ppermute | solution.py:297
  679.2 59.0 %collective-permute-start.31 = (bf16[64,3072]{1,0:T(8,128)(2,1)}, bf16[64,3072]{1,0:T(8,128)(2,1)}, u32[]{:S(2)}, u32[]{:S(2)}) collective-permute-start(bf16[64,3072]{1,0:T(8,128)(2,1)} %get-tuple-element.67), channel_id=1, source_target_pairs={{31,27},{30,26},{29,25},{28,24},{27,23},{26,22},{25,21},{24,20}} | collective-permute-start | bytes 1179656 | tf_op jit(solution)/shard_map/ppermute | solution.py:297
  680.7 127.5 %collective-permute-start.29 = (bf16[64,3072]{1,0:T(8,128)(2,1)}, bf16[64,3072]{1,0:T(8,128)(2,1)}, u32[]{:S(2)}, u32[]{:S(2)}) collective-permute-start(bf16[64,3072]{1,0:T(8,128)(2,1)} %get-tuple-element.66), channel_id=1, source_target_pairs={{16,20},{17,21},{18,22},{19,23},{20,24},{21,25},{22,26},{23,27},{2... | collective-permute-start | bytes 1179656 | tf_op jit(solution)/shard_map/ppermute | solution.py:297
  760.9 47.9 %collective-permute-start.32 = (bf16[64,3072]{1,0:T(8,128)(2,1)S(1)}, bf16[64,3072]{1,0:T(8,128)(2,1)S(1)}, u32[]{:S(2)}, u32[]{:S(2)}) collective-permute-start(bf16[64,3072]{1,0:T(8,128)(2,1)S(1)} %fusion.136), channel_id=1, source_target_pairs={{31,27},{30,26},{29,25},{28,24},{27,23},{26,22},{25,21},{24,20},{2... | collective-permute-start | bytes 1179656 | tf_op jit(solution)/shard_map/ppermute | solution.py:297
  762.5 48.5 %collective-permute-start.17 = (bf16[64,3072]{1,0:T(8,128)(2,1)S(1)}, bf16[64,3072]{1,0:T(8,128)(2,1)S(1)}, u32[]{:S(2)}, u32[]{:S(2)}) collective-permute-start(bf16[64,3072]{1,0:T(8,128)(2,1)S(1)} %get-tuple-element.62), channel_id=1, source_target_pairs={{0,4},{1,5},{2,6},{3,7},{4,8},{5,9},{6,10},{7,11},{8,12},{9,13},{1... | collective-permute-start | bytes 1179656 | tf_op jit(solution)/shard_map/ppermute | solution.py:297
  811.0 44.9 %collective-permute-start.77 = (bf16[64,4096]{1,0:T(8,128)(2,1)S(1)}, bf16[64,4096]{1,0:T(8,128)(2,1)S(1)}, u32[]{:S(2)}, u32[]{:S(2)}) collective-permute-start(bf16[64,4096]{1,0:T(8,128)(2,1)S(1)} %get-tuple-element.58), channel_id=1, source_target_pairs={{16,20},{17,21},{18,22},{19,23},{20,24},{21,25},{22,26},{23,27},{2... | collective-permute-start | bytes 1572872 | tf_op jit(solution)/shard_map/ppermute | solution.py:297
  816.2 39.6 %collective-permute-start.65 = (bf16[64,4096]{1,0:T(8,128)(2,1)S(1)}, bf16[64,4096]{1,0:T(8,128)(2,1)S(1)}, u32[]{:S(2)}, u32[]{:S(2)}) collective-permute-start(bf16[64,4096]{1,0:T(8,128)(2,1)S(1)} %get-tuple-element.54), channel_id=1, source_target_pairs={{0,4},{1,5},{2,6},{3,7},{4,8},{5,9},{6,10},{7,11},{8,12},{9,13},{1... | collective-permute-start | bytes 1572872 | tf_op jit(solution)/shard_map/ppermute | solution.py:297
  (222 other events, 3030.6 us)

commit v2 on v1

v2 whole, which is shorter than its diff:
```python
import functools

import jax
import jax.numpy as jnp
from jax import lax
from jax.experimental import pallas as pl
from jax.experimental.pallas import tpu as pltpu
from jax.sharding import PartitionSpec as P

HEADS = 16
EPSILON = 1e-05
BF16 = jnp.bfloat16
F32 = jnp.float32
VMEM_LIMIT = 48 * 1024 * 1024
CHUNK = 128
UNIT = 256


def dot(left, right):
    return jnp.dot(left, right, preferred_element_type=F32)


def dot_t(left, right):
    return lax.dot_general(left, right, (((1,), (1,)), ((), ())), preferred_element_type=F32)


def t_dot(left, right):
    return lax.dot_general(left, right, (((0,), (0,)), ((), ())), preferred_element_type=F32)


def add_all(terms):
    return functools.reduce(lambda s, t: s + t, terms)


def whole(shape):
    return pl.BlockSpec(shape, lambda *_: (0,) * len(shape))


def params():
    return pltpu.CompilerParams(vmem_limit_bytes=VMEM_LIMIT)


def sds(shape, dtype=BF16):
    return jax.ShapeDtypeStruct(shape, dtype)


def cost(flops, size):
    return pl.CostEstimate(flops=flops, bytes_accessed=size, transcendentals=0)


def weight_specs(weight, block, index):
    if not isinstance(weight, tuple):
        return [pl.BlockSpec(block, index)], [weight]

    def spec(place):
        def at(j, s):
            return tuple(jnp.where(s[0] == place, i, 0) for i in index(j, s))

        return pl.BlockSpec(block, at)

    return [spec(0), spec(1)], list(weight)


def read(core, refs):
    if len(refs) == 1:
        return refs[0][...]
    return jnp.where(core == 0, refs[0][...], refs[1][...])


def layer_call(kernel, name, core, grid, operands, outs, scratch, flops):
    specs, arrays, counts = [], [], []
    for operand in operands:
        if len(operand) == 3:
            more, given = weight_specs(*operand)
        else:
            more, given = [operand[1]], [operand[0]]
        specs, arrays = specs + more, arrays + given
        counts.append(len(given))

    def body(core_ref, *refs):
        refs, groups = list(refs), []
        for count in counts:
            groups.append(refs[:count])
            refs = refs[count:]
        kernel(core_ref[0], groups, *refs)

    size = sum(a.size * a.dtype.itemsize for a in arrays)
    size += sum(o.size * o.dtype.itemsize for o, _ in outs)
    return pl.pallas_call(
        body,
        grid_spec=pltpu.PrefetchScalarGridSpec(
            num_scalar_prefetch=1,
            grid=(grid,),
            in_specs=specs,
            out_specs=[spec for _, spec in outs],
            scratch_shapes=scratch,
        ),
        out_shape=[o for o, _ in outs],
        compiler_params=params(),
        cost_estimate=cost(flops, size),
        name=name,
    )(core, *arrays)


def rstd(rows):
    return lax.rsqrt(jnp.mean(rows * rows, axis=-1, keepdims=True) + EPSILON)


def by_chunks(rows, step):
    def one(i, carry):
        step(pl.ds(pl.multiple_of(i * CHUNK, CHUNK), CHUNK))
        return carry

    lax.fori_loop(0, rows // CHUNK, one, 0)


def norm_backward(grad, rows, gain):
    scale = rstd(rows)
    plain = rows * scale
    grad_gain = jnp.sum(grad * plain, axis=0, keepdims=True)
    lead = grad * gain
    return scale * (lead - plain * jnp.mean(lead * plain, axis=-1, keepdims=True)), grad_gain


def gelu_parts(hidden):
    c = 0.7978845608028654
    square = hidden * hidden
    t = jnp.tanh(hidden * (c + (c * 0.044715) * square))
    half = 0.5 + 0.5 * t
    slope = half + (hidden * half) * ((1.0 - t) * (c + (3 * 0.044715 * c) * square))
    return (hidden * half).astype(BF16), slope.astype(BF16)


def qkv_forward(core, rows, gain, w_qkv, tile=1024):
    count, features = rows.shape
    wide = 3 * features

    def kernel(core, ins, h_ref, p_ref):
        (x_ref,), gain_refs, w_refs = ins

        @pl.when(pl.program_id(0) == 0)
        def _():
            gain = read(core, gain_refs)

            def step(at):
                x = x_ref[at, :]
                h_ref[at, :] = (x * rstd(x) * gain).astype(BF16)

            by_chunks(count, step)

        p_ref[...] = dot(h_ref[...], read(core, w_refs)).astype(BF16)

    return layer_call(
        kernel,
        "qkv_forward",
        core,
        wide // tile,
        [
            (rows, whole(rows.shape)),
            (gain, (1, features), lambda j, s: (0, 0)),
            (w_qkv, (features, tile), lambda j, s: (0, j)),
        ],
        [
            (sds(rows.shape), whole(rows.shape)),
            (sds((count, wide)), pl.BlockSpec((count, tile), lambda j, s: (0, j))),
        ],
        [],
        2 * count * features * wide,
    )


def mlp_forward(core, rows, mixture, w_out, gain, w_up, w_down, joined, tile=1024):
    count, features = rows.shape
    wide = (w_up[0] if isinstance(w_up, tuple) else w_up).shape[1]

    def kernel(core, ins, m_ref, h_ref, *refs):
        (x_ref,), (o_ref,), wout_refs, gain_refs, wup_refs, wdown_refs = ins
        y_ref, acc_ref = refs[-2:]

        @pl.when(pl.program_id(0) == 0)
        def _():
            gain, w_out = read(core, gain_refs), read(core, wout_refs)

            def step(at):
                m = x_ref[at, :] + dot(o_ref[at, :], w_out)
                m_ref[at, :] = m
                acc_ref[at, :] = m
                h_ref[at, :] = (m * rstd(m) * gain).astype(BF16)

            by_chunks(count, step)

        g, slope = gelu_parts(dot(h_ref[...], read(core, wup_refs)))
        if joined:
            refs[0][0] = g
            refs[0][1] = slope
        else:
            refs[0][0] = g
            refs[1][0] = slope
        acc_ref[...] += dot(g, read(core, wdown_refs))

        @pl.when(pl.program_id(0) == pl.num_programs(0) - 1)
        def _():
            y_ref[...] = acc_ref[...].astype(BF16)

    planes = 2 if joined else 1
    wide_out = (sds((planes, count, wide)), pl.BlockSpec((planes, count, tile), lambda j, s: (0, 0, j)))
    same = whole(rows.shape)
    return layer_call(
        kernel,
        "mlp_forward",
        core,
        wide // tile,
        [
            (rows, same),
            (mixture, same),
            (w_out, (features, features), lambda j, s: (0, 0)),
            (gain, (1, features), lambda j, s: (0, 0)),
            (w_up, (features, tile), lambda j, s: (0, j)),
            (w_down, (tile, features), lambda j, s: (j, 0)),
        ],
        [(sds(rows.shape, F32), same), (sds(rows.shape), same)]
        + [wide_out] * (3 - planes)
        + [(sds(rows.shape), same)],
        [pltpu.VMEM(rows.shape, F32)],
        2 * count * features * (features + 2 * wide),
    )


def mlp_backward(core, low_out, slope, middle, w_out, gain, w_up, w_down, tile=1024):
    count, features = low_out.shape
    wide = slope[0].shape[2]
    tiles = wide // tile
    half = tiles // 2

    def kernel(core, ins, own_ref, other_ref, dm_ref, low_ref, do_ref, gg_ref, acc_ref):
        (dy_ref,), (s_ref,), (m_ref,), gain_refs, wdown_refs, wup_refs, wout_refs = ins
        j = pl.program_id(0)
        dz = (s_ref[0].astype(F32) * dot_t(dy_ref[...], read(core, wdown_refs))).astype(BF16)

        @pl.when(j < half)
        def _():
            other_ref[0] = dz

        @pl.when(j >= half)
        def _():
            own_ref[0] = dz

        term = dot_t(dz, read(core, wup_refs))

        @pl.when(j == 0)
        def _():
            acc_ref[...] = term

        @pl.when(j > 0)
        def _():
            acc_ref[...] += term

        @pl.when(j == tiles - 1)
        def _():
            gg_ref[...] = jnp.zeros_like(gg_ref)
            gain, w_out = read(core, gain_refs), read(core, wout_refs)

            def step(at):
                dm, gg = norm_backward(acc_ref[at, :], m_ref[0, at, :].astype(F32), gain)
                gg_ref[...] += gg
                dm = dm + dy_ref[at, :].astype(F32)
                dm_ref[at, :] = dm
                low = dm.astype(BF16)
                low_ref[at, :] = low
                do_ref[at, :] = dot_t(low, w_out).astype(BF16)

            by_chunks(count, step)

    def at(j, s):
        return (j + (1 - s[0]) * half) % tiles

    same = whole(low_out.shape)
    return layer_call(
        kernel,
        "mlp_backward",
        core,
        tiles,
        [
            (low_out, same),
            (
                slope[0],
                pl.BlockSpec(
                    (1, count, tile), lambda j, s: (slope[1], s[0] * slope[2], at(j, s))
                ),
            ),
            (
                middle[0],
                pl.BlockSpec(
                    (1, count, features), lambda j, s: (middle[1], s[0] * middle[2], 0)
                ),
            ),
            (gain, (1, features), lambda j, s: (0, 0)),
            (w_down, (tile, features), lambda j, s: (at(j, s), 0)),
            (w_up, (features, tile), lambda j, s: (0, at(j, s))),
            (w_out, (features, features), lambda j, s: (0, 0)),
        ],
        [
            (
                sds((1, count, wide // 2)),
                pl.BlockSpec((1, count, tile), lambda j, s: (0, 0, jnp.maximum(j - half, 0))),
            ),
            (
                sds((1, count, wide // 2)),
                pl.BlockSpec((1, count, tile), lambda j, s: (0, 0, jnp.minimum(j, half - 1))),
            ),
            (sds(low_out.shape, F32), same),
            (sds(low_out.shape), same),
            (sds(low_out.shape), same),
            (sds((1, features), F32), whole((1, features))),
        ],
        [pltpu.VMEM(low_out.shape, F32)],
        2 * count * features * (features + 2 * wide),
    )


def qkv_backward(core, own, other, rows, grad_middle, gain, w_qkv, books, tile=512):
    count, features = rows.shape
    frames = count // books

    def kernel(core, ins, dx_ref, sum_ref, gg_ref, acc_ref):
        (own_ref,), (other_ref,), (x_ref,), (dm_ref,), gain_refs, w_refs = ins
        w = read(core, w_refs)
        j = pl.program_id(0)
        terms = []
        for i in range(3):
            part = jnp.where(core == i // 2, own_ref[i % 2], other_ref[i % 2])
            terms.append(dot_t(part, w[:, i * features : (i + 1) * features]))
        acc_ref[:, pl.ds(pl.multiple_of(j * tile, tile), tile)] = add_all(terms)

        @pl.when(j == pl.num_programs(0) - 1)
        def _():
            gg_ref[...] = jnp.zeros_like(gg_ref)
            gain = read(core, gain_refs)
            total = 0.0
            for b in range(books):
                at = slice(b * frames, (b + 1) * frames)
                dx, gg = norm_backward(acc_ref[at, :], x_ref[at, :], gain)
                gg_ref[...] += gg
                dx = dx + dm_ref[at, :]
                dx_ref[at, :] = dx
                total = total + dx
            sum_ref[...] = total.astype(BF16)

    same = whole(rows.shape)
    return layer_call(
        kernel,
        "qkv_backward",
        core,
        features // tile,
        [
            (own, whole(own.shape)),
            (other, whole(other.shape)),
            (rows, same),
            (grad_middle, same),
            (gain, (1, features), lambda j, s: (0, 0)),
            (w_qkv, (tile, 3 * features), lambda j, s: (j, 0)),
        ],
        [
            (sds(rows.shape, F32), same),
            (sds((frames, features)), whole((frames, features))),
            (sds((1, features), F32), whole((1, features))),
        ],
        [pltpu.VMEM(rows.shape, F32)],
        6 * count * features * features,
    )


def head_sum(product, reduce_mat):
    high = product.astype(BF16)
    low = (product - high.astype(F32)).astype(BF16)
    return dot(high, reduce_mat) + dot(low, reduce_mat)


def head_mats(lanes, width):
    row = lax.broadcasted_iota(jnp.int32, (lanes, 128), 0)
    col = lax.broadcasted_iota(jnp.int32, (lanes, 128), 1)
    reduce_mat = (row // width == col).astype(BF16)
    row = lax.broadcasted_iota(jnp.int32, (128, lanes), 0)
    col = lax.broadcasted_iota(jnp.int32, (128, lanes), 1)
    return reduce_mat, (col // width == row).astype(BF16)


def local_probs(q, k, reduce_mat, scale):
    probs = {}
    for a in range(len(q)):
        scores = [head_sum(q[a] * k[b], reduce_mat) * scale for b in range(a + 1)]
        peak = functools.reduce(jnp.maximum, scores)
        parts = [jnp.exp(s - peak) for s in scores]
        total = add_all(parts)
        for b in range(a + 1):
            probs[a, b] = parts[b] / total
    return probs


def local_attn_fwd_kernel(width, q_ref, k_ref, v_ref, o_ref):
    books, _, lanes = q_ref.shape
    reduce_mat, expand_mat = head_mats(lanes, width)
    q = [q_ref[a].astype(F32) for a in range(books)]
    k = [k_ref[a].astype(F32) for a in range(books)]
    v = [v_ref[a].astype(F32) for a in range(books)]
    probs = local_probs(q, k, reduce_mat, width**-0.5)
    for a in range(books):
        mixed = [dot(probs[a, b].astype(BF16), expand_mat) * v[b] for b in range(a + 1)]
        o_ref[a] = add_all(mixed).astype(BF16)


def by_half(core, parts, own_ref, other_ref):
    for c in range(2):

        @pl.when(core == c)
        def _():
            for i in range(2):
                own_ref[i] = parts[2 * c + i]
                other_ref[i] = parts[2 - 2 * c + i]


def local_attn_bwd_kernel(
    width, core_ref, q_ref, k_ref, v_ref, g_ref, m_ref, own_ref, other_ref
):
    books, _, lanes = q_ref.shape
    scale = width**-0.5
    reduce_mat, expand_mat = head_mats(lanes, width)
    q = [q_ref[a].astype(F32) for a in range(books)]
    k = [k_ref[a].astype(F32) for a in range(books)]
    v = [v_ref[a].astype(F32) for a in range(books)]
    g = [g_ref[a].astype(F32) for a in range(books)]
    probs = local_probs(q, k, reduce_mat, scale)
    dq = [0.0] * books
    dk = [0.0] * books
    dv = [0.0] * books
    for a in range(books):
        dprobs = [head_sum(g[a] * v[b], reduce_mat) for b in range(a + 1)]
        inner = add_all([dprobs[b] * probs[a, b] for b in range(a + 1)])
        for b in range(a + 1):
            dscore = dot((probs[a, b] * (dprobs[b] - inner)).astype(BF16), expand_mat)
            dq[a] = dq[a] + dscore * k[b]
            dk[b] = dk[b] + dscore * q[a]
            dv[b] = dv[b] + dot(probs[a, b].astype(BF16), expand_mat) * g[a]
    parts = [
        jnp.stack([(one * by).astype(BF16) for one in ones])
        for ones, by in ((dq, scale), (dk, scale), (dv, 1.0))
    ]
    by_half(core_ref[0], parts + [m_ref[...]], own_ref, other_ref)


def local_attn(packed, books, core=None, grads=None, lanes=256):
    count, wide = packed.shape
    features, frames = wide // 3, count // books
    width, groups = features // HEADS, features // lanes
    packed = packed.reshape(books, frames, wide)
    shape = (books, frames, features)

    def spec(part):
        return pl.BlockSpec((books, frames, lanes), lambda h, *_: (0, 0, part * groups + h))

    ins = [spec(0), spec(1), spec(2)]
    if grads is None:
        out = pl.pallas_call(
            functools.partial(local_attn_fwd_kernel, width),
            grid=(groups,),
            in_specs=ins,
            out_specs=spec(0),
            out_shape=sds(shape),
            compiler_params=params(),
            cost_estimate=cost(2000 * count * features, 8 * count * features),
            name="local_attn_forward",
        )(packed, packed, packed)
        return out.reshape(count, features)
    half = pl.BlockSpec((2, books, frames, lanes), lambda h, _: (0, 0, 0, h))
    out = pl.pallas_call(
        functools.partial(local_attn_bwd_kernel, width),
        grid_spec=pltpu.PrefetchScalarGridSpec(
            num_scalar_prefetch=1,
            grid=(groups,),
            in_specs=ins + [spec(0)] * 2,
            out_specs=[half] * 2,
        ),
        out_shape=[sds((2,) + shape)] * 2,
        compiler_params=params(),
        cost_estimate=cost(4000 * count * features, 16 * count * features),
        name="local_attn_backward",
    )(core, packed, packed, packed, grads[0].reshape(shape), grads[1].reshape(shape))
    return [one.reshape(2, count, features) for one in out]


def item_mask(lengths_ref, micro, frames, items):
    row = lax.broadcasted_iota(jnp.int32, (frames, frames), 0)
    col = lax.broadcasted_iota(jnp.int32, (frames, frames), 1)
    row_item = jnp.zeros((frames, frames), jnp.int32)
    col_item = jnp.zeros((frames, frames), jnp.int32)
    end = 0
    for i in range(items):
        end = end + lengths_ref[micro, 0, i]
        row_item = row_item + (row >= end).astype(jnp.int32)
        col_item = col_item + (col >= end).astype(jnp.int32)
    return (row_item == col_item) & (row >= col)


def head_parts(block, width):
    per = 128 // width
    lane = lax.broadcasted_iota(jnp.int32, (block.shape[0], 128), 1)
    parts = []
    for h in range(block.shape[1] // width):
        tile = block[:, (h // per) * 128 : (h // per + 1) * 128]
        parts.append(jnp.where(lane // width == h % per, tile, jnp.zeros_like(tile)))
    return parts


def frame_probs(q, k, mask, scale):
    scores = jnp.where(mask, dot_t(q, k) * scale, -1e30)
    parts = jnp.exp(scores - jnp.max(scores, axis=-1, keepdims=True))
    return parts / jnp.sum(parts, axis=-1, keepdims=True)


def global_attn_fwd_kernel(width, items, lengths_ref, q_ref, k_ref, v_ref, o_ref):
    frames, lanes = q_ref.shape
    mask = item_mask(lengths_ref, pl.program_id(0), frames, items)
    per = 128 // width
    q = head_parts(q_ref[...], width)
    v = head_parts(v_ref[...], width)
    mixed = [0.0] * (lanes // 128)
    for h in range(lanes // width):
        tile = slice((h // per) * 128, (h // per + 1) * 128)
        probs = frame_probs(q[h], k_ref[:, tile], mask, width**-0.5)
        mixed[h // per] = mixed[h // per] + dot(probs.astype(BF16), v[h])
    for i, tile in enumerate(mixed):
        o_ref[:, i * 128 : (i + 1) * 128] = tile.astype(BF16)


def global_attn_bwd_kernel(
    width, items, core_ref, lengths_ref, q_ref, k_ref, v_ref, g_ref, m_ref, own_ref, other_ref
):
    frames, lanes = q_ref.shape
    scale = width**-0.5
    mask = item_mask(lengths_ref, core_ref[0], frames, items)
    per = 128 // width
    q = head_parts(q_ref[...], width)
    k = head_parts(k_ref[...], width)
    g = head_parts(g_ref[...], width)
    tiles = lanes // 128
    dq, dk, dv = [0.0] * tiles, [0.0] * tiles, [0.0] * tiles
    for h in range(lanes // width):
        t = h // per
        tile = slice(t * 128, (t + 1) * 128)
        probs = frame_probs(q[h], k_ref[:, tile], mask, scale)
        dv[t] = dv[t] + t_dot(probs.astype(BF16), g[h])
        dprobs = dot_t(g[h], v_ref[:, tile])
        inner = jnp.sum(dprobs * probs, axis=-1, keepdims=True)
        dscore = (probs * (dprobs - inner)).astype(BF16)
        dq[t] = dq[t] + dot(dscore, k[h])
        dk[t] = dk[t] + t_dot(dscore, q[h])
    parts = [
        jnp.concatenate([(one * by).astype(BF16) for one in ones], axis=1)
        for ones, by in ((dq, scale), (dk, scale), (dv, 1.0))
    ]
    by_half(core_ref[0], parts + [m_ref[...]], own_ref, other_ref)


def global_attn_forward(packed, lengths, lanes=512):
    micros, _, items = lengths.shape
    count, wide = packed.shape
    features, frames = wide // 3, count // micros
    width, groups = features // HEADS, features // lanes

    def spec(part):
        return pl.BlockSpec((frames, lanes), lambda m, h, _: (m, part * groups + h))

    return pl.pallas_call(
        functools.partial(global_attn_fwd_kernel, width, items),
        grid_spec=pltpu.PrefetchScalarGridSpec(
            num_scalar_prefetch=1,
            grid=(micros, groups),
            in_specs=[spec(0), spec(1), spec(2)],
            out_specs=spec(0),
        ),
        out_shape=sds((count, features)),
        compiler_params=params(),
        cost_estimate=cost(3000 * count * features, 8 * count * features),
        name="global_attn_forward",
    )(lengths, packed, packed, packed)


def global_attn_backward(core, kept, first, lengths, grads, lanes=512):
    micros, _, items = lengths.shape
    _, count, features = kept.shape
    frames = count // micros
    width, groups = features // HEADS, features // lanes

    def spec(part):
        return pl.BlockSpec((None, frames, lanes), lambda h, c, _: (first + part, c[0], h))

    own = pl.BlockSpec((frames, lanes), lambda h, *_: (0, h))
    half = pl.BlockSpec((2, frames, lanes), lambda h, *_: (0, 0, h))
    return pl.pallas_call(
        functools.partial(global_attn_bwd_kernel, width, items),
        grid_spec=pltpu.PrefetchScalarGridSpec(
            num_scalar_prefetch=2,
            grid=(groups,),
            in_specs=[spec(0), spec(1), spec(2), own, own],
            out_specs=[half] * 2,
        ),
        out_shape=[sds((2, frames, features))] * 2,
        compiler_params=params(),
        cost_estimate=cost(4000 * frames * features, 16 * frames * features),
        name="global_attn_backward",
    )(core, lengths, kept, kept, kept, *grads)


def place_columns(arrays, spots):
    shape = arrays[0].shape

    def kernel(s_ref, *refs):
        for i in range(len(arrays)):
            refs[-1][i] = dot(refs[i][...], s_ref[...]).astype(BF16)

    return pl.pallas_call(
        kernel,
        out_shape=sds((len(arrays),) + shape),
        compiler_params=params(),
        cost_estimate=cost(
            2 * len(arrays) * shape[0] * shape[1] ** 2, 4 * len(arrays) * arrays[0].size
        ),
        name="place_columns",
    )(spots, *arrays)


def pack(arrays, features):
    count = arrays[0].shape[0]
    planes = [(i, c) for i, a in enumerate(arrays) for c in range(a.shape[1] // features)]

    def kernel(*refs):
        for plane, (i, c) in enumerate(planes):
            refs[-1][plane] = refs[i][:, c * features : (c + 1) * features].astype(BF16)

    return pl.pallas_call(
        kernel,
        out_shape=sds((len(planes), count, features)),
        compiler_params=params(),
        cost_estimate=cost(0, 4 * len(planes) * count * features),
        name="pack",
    )(*arrays)


class Group:
    def __init__(self, table, units, lefts, rights, tile, tiles, across):
        self.table, self.per = table, units // 4
        self.lefts, self.rights = lefts, rights
        self.tile, self.tiles, self.across = tile, tiles, across


def weight_grad(group, table, first, steps, per, addends, split):
    lefts, rights, tile = group.lefts, group.rights, group.tile
    ordered = len(lefts) == 1 or len(rights) == 1
    count = sum(a.shape[1] for a, _ in lefts)

    def joined(core, blocks):
        if len(blocks) == 1:
            return blocks[0]
        a, b = blocks
        if ordered:
            a, b = jnp.where(core == 0, a, b), jnp.where(core == 0, b, a)
        return jnp.concatenate([a, b], axis=0)

    def kernel(table_ref, *refs):
        core, refs = table_ref[0], list(refs)
        left_refs = [refs[i * per : (i + 1) * per] for i in range(len(lefts))]
        refs = refs[len(lefts) * per :]
        right = joined(core, [r[0] for r in refs[: len(rights)]])
        add_refs = refs[len(rights) : len(rights) + len(addends)]
        out_refs = refs[len(rights) + len(addends) :]
        for i in range(per):
            at = slice(i * UNIT, (i + 1) * UNIT)
            left = joined(core, [r[i][0] for r in left_refs])
            out = add_all([t_dot(left, right)] + [r[at, :].astype(F32) for r in add_refs])
            out = out.astype(BF16)
            if not split:
                out_refs[0][at, :] = out
            elif per == 1:
                out_refs[0][...] = out[: UNIT // 2]
                out_refs[1][...] = out[UNIT // 2 :]
            else:
                half = per // 2
                out_refs[i // half][(i % half) * UNIT : (i % half + 1) * UNIT, :] = out

    def left_spec(start, rows, i):
        return pl.BlockSpec(
            (1, rows, UNIT),
            lambda u, j, t: (group.across(j, t)[0], 0, t[start + first + u * per + i]),
        )

    def right_spec(rows):
        return pl.BlockSpec(
            (1, rows, tile), lambda u, j, t: (group.across(j, t)[1], 0, group.across(j, t)[2])
        )

    def block(skip, rows=per * UNIT):
        return pl.BlockSpec((rows, tile), lambda u, j, t: (skip + u, j))

    wide = group.tiles * tile
    if split:
        outs = [sds((per * UNIT // 2, wide))] * 2
        out_specs = [block(0, per * UNIT // 2)] * 2
    else:
        outs, out_specs = [sds((steps * per * UNIT, wide))], [block(0)]
    size = steps * per * UNIT * wide
    out = pl.pallas_call(
        kernel,
        grid_spec=pltpu.PrefetchScalarGridSpec(
            num_scalar_prefetch=1,
            grid=(steps, group.tiles),
            in_specs=[left_spec(start, a.shape[1], i) for a, start in lefts for i in range(per)]
            + [right_spec(a.shape[1]) for a in rights]
            + [block(skip) for _, skip in addends],
            out_specs=out_specs,
        ),
        out_shape=outs,
        compiler_params=params(),
        cost_estimate=cost(
            2 * count * size, 2 * (count * (steps * per * UNIT + wide) + size * (1 + len(addends)))
        ),
        name="weight_grad",
    )(table, *[a for a, _ in lefts for _ in range(per)], *rights, *[a for a, _ in addends])
    return out if split else out[0]


class Devices:
    def __init__(self, size):
        self.size = size
        self.core = lax.axis_index("section")
        self.index = lax.axis_index("dp")

    def bits(self, core, late):
        near = [1, 2] if core == 0 else [2, 1]
        far = [1 << b for b in range(2, self.size.bit_length() - 1)]
        return far + near if late else near + far

    def swap(self, array, step, late=False):
        pairs = []
        for core in range(2):
            by = self.bits(core, late)[step]
            pairs += [(core * self.size + i, core * self.size + (i ^ by)) for i in range(self.size)]
        return lax.ppermute(array, ("section", "dp"), pairs)

    def cores(self, array):
        return lax.ppermute(array, "section", [(0, 1), (1, 0)])

    def order(self, late=False):
        orders = []
        for core in range(2):
            bits = self.bits(core, late)
            order = [
                sum(bit for i, bit in enumerate(bits) if (spot >> (len(bits) - 1 - i)) & 1)
                for spot in range(self.size)
            ]
            orders.append(jnp.array(order, jnp.int32))
        return jnp.where(self.core == 0, orders[0], orders[1]) ^ self.index

    def columns(self, count, late=False):
        block = count // self.size
        order = self.order(late)
        return (order[:, None] * block + jnp.arange(block, dtype=jnp.int32)).reshape(-1)

    def spots(self, count):
        at = self.columns(count)[None, :]
        return (lax.broadcasted_iota(jnp.int32, (count, count), 0) == at).astype(BF16)

    def table(self, *orders):
        parts = [self.core[None].astype(jnp.int32)] + [jnp.asarray(o, jnp.int32) for o in orders]
        return jnp.concatenate(parts)

    def total(self, array):
        for step in range(self.size.bit_length() - 1):
            array = array + self.swap(array, step)
        return array


class Sum:
    def __init__(self, devices, line, group, late=False):
        self.devices, self.line, self.group, self.late = devices, line, group, late
        self.step = 0

    def grad(self, first, count, addends, split=False):
        group = self.group
        steps, per = (count, group.per) if group.per > 1 else (1, count)
        out = weight_grad(
            group, self.line.tie(group.table), first * group.per, steps, per, addends, split
        )
        self.line.mark(out[0] if split else out)
        return out

    def send(self, array):
        got = self.devices.swap(array, self.step, self.late)
        self.step += 1
        return got

    def first(self):
        self.one = self.send(self.grad(2, 2, []))

    def second(self):
        skip = 1
        self.two = self.send(self.grad(1, 1, [(self.one, skip)]))

    def third(self):
        self.kept, sent = self.grad(0, 1, [(self.one, 0), (self.two, 0)], split=True)
        self.got = self.send(sent)

    def last(self):
        total = self.kept
        steps = self.devices.size.bit_length() - 1
        while self.step < steps:
            half = total.shape[0] // 2
            sent = (total[half:].astype(F32) + self.got[half:].astype(F32)).astype(BF16)
            total = total[:half].astype(F32) + self.got[:half].astype(F32)
            if self.step < steps - 1:
                total = total.astype(BF16)
            self.got = self.send(sent)
        return total.astype(F32) + self.got.astype(F32)


class Line:
    def __init__(self):
        self.token = None

    def tie(self, table):
        if self.token is None:
            return table
        return lax.optimization_barrier((table, self.token))[0]

    def mark(self, token):
        self.token = token


def local(codebook_embed, item_lengths, gain_attn, w_qkv, w_out, gain_mlp, w_up, w_down, cotangent):
    size = lax.axis_size("dp")
    micros, frames, books, features = codebook_embed.shape
    half_width = features // 2
    scale_in = books**-0.5
    devices, line = Devices(size), Line()
    core = devices.core
    first_core = core == 0
    here = core[None].astype(jnp.int32)

    def run(kernel, *operands):
        out = kernel(line.tie(here), *operands)
        line.mark(out[0])
        return out

    gains = jnp.stack([gain_attn[0], gain_mlp[0]])
    own = [w_qkv[0], w_out[0], w_up[0], w_down[0]]
    gains_other = devices.cores(gains)
    other = [devices.cores(w) for w in own]
    global_weights = list(zip(own, other))
    local_weights = list(zip(other, own))
    global_gains = [(gains[i : i + 1], gains_other[i : i + 1]) for i in range(2)]
    local_gains = [(b, a) for a, b in global_gains]

    embed_all = codebook_embed.transpose(0, 2, 1, 3)
    frame_in = jnp.sum(embed_all.astype(F32), axis=1) * scale_in
    rows = frame_in.reshape(-1, features)
    normed, packed = run(qkv_forward, rows, gains[:1], own[0])
    mixture = global_attn_forward(packed, item_lengths)
    line.mark(mixture)
    middle, normed_two, active, result = run(
        lambda c: mlp_forward(c, rows, mixture, own[1], gains[1:], own[2], own[3], True)
    )

    def from_first(array):
        return lax.ppermute(array, "section", [(0, 1)])

    states = jnp.where(first_core, result[:frames], from_first(result[frames:]))
    kept = pack([normed, mixture, normed_two, packed, middle], features)
    kept = jnp.where(first_core, kept, from_first(kept))
    active = jnp.where(first_core, active, from_first(active))

    embed = lax.dynamic_index_in_dim(embed_all, core, 0, keepdims=False)
    frame_rows = lax.dynamic_index_in_dim(frame_in, core, 0, keepdims=False)
    local_rows = (embed.astype(F32) + states.astype(F32)[None]).reshape(-1, features)
    w_qkv_l, w_out_l, w_up_l, w_down_l = local_weights
    l_normed, l_packed = run(qkv_forward, local_rows, local_gains[0], w_qkv_l)
    l_mixture = local_attn(l_packed, books)
    line.mark(l_mixture)
    l_middle, l_normed_two, l_active, l_slope, l_out = run(
        lambda c: mlp_forward(
            c, local_rows, l_mixture, w_out_l, local_gains[1], w_up_l, w_down_l, False
        )
    )

    unit_rows = w_down.shape[1] // size == UNIT
    same = [0, 1, 2, 3]
    placed_table = devices.table(same, [0, 2, 1, 3])
    spots = devices.spots(features)

    def down_group(lefts, rights, late):
        if unit_rows:
            table = devices.table(devices.order(late))
        else:
            table = devices.table(range(lefts[0].shape[2] // UNIT))
            order = devices.columns(lefts[0].shape[2], late)
            lefts = [jnp.take(a[:1], order, axis=2) for a in lefts]
        units = lefts[0].shape[2] // UNIT
        return Group(
            table, units, [(a, 1) for a in lefts], rights, half_width, 1, lambda j, t: (0, 0, 0)
        )

    def up_group(lefts, rights):
        return Group(placed_table, 4, lefts, rights, features, 2, lambda j, t: (2, 0, j))

    def rest_group(lefts, rights):
        def across(j, t):
            return jnp.where(2 * t[0] + j == 3, 1, 0), j, 0

        return Group(placed_table, 4, lefts, rights, features, 2, across)

    def my_half(array):
        return jnp.where(first_core, array[..., :half_width], array[..., half_width:])

    def other_half(array):
        return jnp.where(first_core, array[..., half_width:], array[..., :half_width])

    upstream_all = cotangent.transpose(0, 2, 1, 3).reshape(micros, -1, features)
    upstream = lax.dynamic_index_in_dim(upstream_all, core, 0, keepdims=False)
    upstream_halves = my_half(upstream_all)
    l_active_got = devices.cores(l_active)
    l_placed = place_columns([l_normed, l_mixture, l_normed_two], spots)
    line.mark(l_placed)
    l_placed_got = devices.cores(l_placed)
    placed_pair = [(l_placed, 1), (l_placed_got, 5)]
    l_down = Sum(
        devices,
        line,
        down_group(
            [l_active, l_active_got],
            [
                lax.dynamic_index_in_dim(upstream_halves, core, 0),
                lax.dynamic_index_in_dim(upstream_halves, 1 - core, 0),
            ],
            False,
        ),
    )
    l_down.first()
    dz_own, dz_other, l_dm, l_low, l_do, l_gain_two = run(
        lambda c: mlp_backward(
            c, upstream, (l_slope, 0, 0), (l_middle[None], 0, 0), w_out_l, local_gains[1], w_up_l, w_down_l
        )
    )
    l_up = Sum(devices, line, up_group(placed_pair, [dz_own, devices.cores(dz_other)]))
    l_down.second()
    l_up.first()
    dp_own, dp_other = run(lambda c: local_attn(l_packed, books, c, (l_do, l_low)))
    l_rest = Sum(devices, line, rest_group(placed_pair, [dp_own, devices.cores(dp_other)]))
    local_grad, frame_grad, l_gain_one = run(
        lambda c: qkv_backward(
            c, dp_own, dp_other, local_rows, l_dm, local_gains[0], w_qkv_l, books
        )
    )
    l_down.third()
    l_up.second()
    l_rest.first()

    w_qkv_g, w_out_g, w_up_g, w_down_g = global_weights
    g_down = Sum(
        devices,
        line,
        down_group(
            [active],
            [my_half(frame_grad)[None], devices.cores(other_half(frame_grad))[None]],
            True,
        ),
        True,
    )
    dz_own, dz_other, g_dm, g_low, g_do, g_gain_two = run(
        lambda c: mlp_backward(
            c, frame_grad, (active, 1, 1), (kept, 6, 1), w_out_g, global_gains[1], w_up_g, w_down_g
        )
    )
    g_down.first()
    placed = place_columns([kept[0], kept[1], kept[2]], spots)
    g_up = Sum(devices, line, up_group([(placed, 1)], [dz_own, devices.cores(dz_other)]))
    dp_own, dp_other = run(
        lambda c: global_attn_backward(c, kept, 3, item_lengths, (g_do, g_low))
    )
    g_rest = Sum(devices, line, rest_group([(placed, 1)], [dp_own, devices.cores(dp_other)]))
    g_up.first()
    global_grad, _, g_gain_one = run(
        lambda c: qkv_backward(
            c, dp_own, dp_other, frame_rows, g_dm, global_gains[0], w_qkv_g, 1
        )
    )
    g_rest.first()
    l_up.third()
    l_rest.second()
    g_down.second()
    g_up.second()
    l_rest.third()
    g_rest.second()
    g_down.third()
    g_up.third()
    g_rest.third()
    l_down, l_up, l_rest, g_down, g_up, g_rest = [
        one.last() for one in (l_down, l_up, l_rest, g_down, g_up, g_rest)
    ]

    def halves(array):
        got = devices.cores(other_half(array).astype(BF16)).astype(array.dtype)
        mine = my_half(array)
        pair = jnp.where(first_core, jnp.stack([mine, got]), jnp.stack([got, mine]))
        return pair.transpose(0, 2, 1, 3)

    local_out = halves(l_out.reshape(books, frames, features))
    embed_grad = halves(
        local_grad.reshape(books, frames, features) + (global_grad * scale_in)[None]
    )

    def layer_sums(ours, theirs):
        sent = devices.cores(jnp.where(first_core, theirs, ours).astype(BF16)).astype(F32)
        mine = jnp.where(first_core, ours, theirs)
        return jnp.where(
            first_core,
            jnp.concatenate([mine, sent], axis=1),
            jnp.concatenate([sent, mine], axis=1),
        )

    down, up, rest = layer_sums(g_down, l_down), layer_sums(g_up, l_up), layer_sums(g_rest, l_rest)
    gain_sums = devices.total(jnp.concatenate([g_gain_one, g_gain_two, l_gain_one, l_gain_two]))
    gain_sums = gain_sums + devices.cores(gain_sums)
    gain_sums = jnp.where(first_core, gain_sums[:2], gain_sums[2:]).reshape(2, size, -1)
    gain_sums = lax.dynamic_index_in_dim(gain_sums, devices.index, 1, keepdims=False)

    return (
        local_out,
        embed_grad,
        gain_sums[:1],
        rest[None, :, : 3 * features],
        rest[None, :, 3 * features :],
        gain_sums[1:],
        up[None],
        down[None],
    )


def solution(mesh):
    in_specs = (
        P(None, "dp", None, None),
        P(None, "dp", None),
        P("section", None),
        P("section", None, None),
        P("section", None, None),
        P("section", None),
        P("section", None, None),
        P("section", None, None),
        P(None, "dp", None, None),
    )
    out_specs = (
        P(None, "dp", None, "section"),
        P(None, "dp", None, "section"),
        P("section", "dp"),
        P("section", "dp", None),
        P("section", "dp", None),
        P("section", "dp"),
        P("section", "dp", None),
        P("section", "dp", None),
    )
    return jax.shard_map(local, mesh=mesh, in_specs=in_specs, out_specs=out_specs, check_vma=False)
```

time: 869 us -> 443 us (0.51)
  matrix products: 230 us -> 0 us
  starting transfers between devices: 238 us -> 61.6 us
  Pallas kernels: 42.9 us -> 197 us
  local copies, waits for them, and re-layouts: 171 us -> 17.9 us
  other arithmetic: 65.8 us -> 24.2 us
  waiting for transfers between devices: 105 us -> 136 us
    dot_general x86 -> x0, matrix products: 230 us -> none  [the longest x64 102 us: t_dot(): lax.dot_general(left, right, (((0,), (0,)), ((), ())), preferred_element_...]
    ppermute x105 -> x49, starting transfers between devices: 238 us -> 61.6 us  [the longest x28 44.1 us: swap(): return lax.ppermute(array, ('section', 'dp'), pairs)]
    pallas_call x4 -> x33, Pallas kernels: 42.9 us -> 197 us  [the longest x8 93 us: layer_call(): pl.pallas_call(body, grid_spec=pltpu.PrefetchScalarGridSpec(num_scalar_pr...]
    unnamed x300 -> x168, local copies, waits for them, and re-layouts: 81.5 us -> 12.1 us
    dynamic_slice x7 -> x1, local copies, waits for them, and re-layouts: 53.6 us -> 0.05 us  [local(): lax.dynamic_index_in_dim(upstream_halves, 1 - core, 0)]
    ppermute x105 -> x49, waiting for transfers between devices: 105 us -> 136 us  [the longest x28 134 us: swap(): return lax.ppermute(array, ('section', 'dp'), pairs)]
    convert_element_type x45 -> x11, other arithmetic: 34 us -> 4.2 us  [the longest x1 1.31 us: local(): embed.astype(F32) + states.astype(F32)[None]]
    reshape x5 -> x1, local copies, waits for them, and re-layouts: 25.3 us -> 0.08 us  [local(): jnp.where(first_core, gain_sums[:2], gain_sums[2:]).reshape(2, size, -1)]
  transfers between devices with their start and end apart: 105 -> 49, of which waited for: 19 -> 19; matrix products, arithmetic and copies ran while one was open for 30% -> 6% of each run, Pallas kernels for 2% -> 36%
where the time goes in v2:
time: 443 us; the launch traced here: 439 us
  Pallas kernels  197 us (44%)
  waiting for transfers between devices  136 us (31%)
  starting transfers between devices  61.6 us (14%)
  other arithmetic  24.2 us (5%)
  local copies, waits for them, and re-layouts  17.9 us (4%)
    ppermute x28, waiting for transfers between devices, swap(): return lax.ppermute(array, ('section', 'dp'), pairs)  134 us
    pallas_call x8, Pallas kernels, layer_call(): pl.pallas_call(body, grid_spec=pltpu.PrefetchScalarGridSpec(num_scalar_pr...  93 us
    pallas_call x18, Pallas kernels, weight_grad(): pl.pallas_call(kernel, grid_spec=pltpu.PrefetchScalarGridSpec(num_scalar_...  72.9 us
    ppermute x28, starting transfers between devices, swap(): return lax.ppermute(array, ('section', 'dp'), pairs)  44.1 us
    unnamed x168, local copies, waits for them, and re-layouts  12.1 us
    ppermute x3, starting transfers between devices, from_first(): return lax.ppermute(array, 'section', [(0, 1)])  9.99 us
  transfers between devices with their start and end apart: 49, of which 19 were waited for; matrix products, arithmetic and copies ran while one was open for 6% of the time, Pallas kernels for 36%

profile of v2, /device:TPU:0, one launch (start us, length us, event | category | flops | bytes accessed | tf_op | source)
XLA Modules:
  0.0 438.7 jit_solution(17129978564488419821)
XLA Ops:
  5.0 5.0 %qkv_forward.2 = (bf16[256,1024]{1,0:T(8,128)(2,1)S(1)}, bf16[256,3072]{1,0:T(8,128)(2,1)S(1)}) custom-call(s32[1]{0:T(128)} %bitcast.core_ref, f32[256,1024]{1,0:T(8,128)S(1)} %bitcast.82, f32[1,1024]{1,0:T(1,128)S(1)} %copy-done.64, bf16[1024,3072]{1,0:T(8,128)(2,1)} %bitcast.105), custom_call_target="tpu_custom_call" | custom-call | flops 1610612736 | bytes 9441280 | tf_op jit(solution)/shard_map/qkv_forward/pallas_call | solution.py:89
  10.8 7.3 %global_attn_forward.1.refs_1_ = bf16[256,1024]{1,0:T(8,128)(2,1)S(1)} custom-call(s32[2,1,8]{2,1,0:T(1,128)S(1)} %copy-done.65, bf16[256,3072]{1,0:T(8,128)(2,1)S(1)} %get-tuple-element.81.q_ref.k_ref.v_ref.refs_3_, bf16[256,3072]{1,0:T(8,128)(2,1)S(1)} %get-tuple-element.81.q_ref.k_ref.v_ref.refs_3_, ...), custom_call_target="tpu_custom_call" | custom-call | flops 786432000 | bytes 2097152 | tf_op jit(solution)/shard_map/global_attn_forward/pallas_call | solution.py:573
  18.1 12.6 %mlp_forward.2 = (f32[256,1024]{1,0:T(8,128)S(1)}, bf16[256,1024]{1,0:T(8,128)(2,1)S(1)}, bf16[2,256,4096]{2,1,0:T(8,128)(2,1)}, bf16[256,1024]{1,0:T(8,128)(2,1)S(1)}) custom-call(s32[1]{0:T(128)} %bitcast.core_ref, f32[256,1024]{1,0:T(8,128)S(1)} %bitcast.83, bf16[256,1024]{1,0:T(8,128)(2,1)S(1)} %global_attn_forward.1.refs_1_, ...), custom_call_target="tpu_custom_call" | custom-call | flops 4831838208 | bytes 26742784 | tf_op jit(solution)/shard_map/mlp_forward/pallas_call | solution.py:89
  38.7 6.9 %qkv_forward.3 = (bf16[384,1024]{1,0:T(8,128)(2,1)S(1)}, bf16[384,3072]{1,0:T(8,128)(2,1)S(1)}) custom-call(s32[1]{0:T(128)} %bitcast.core_ref, f32[384,1024]{1,0:T(8,128)S(1)} %bitcast_add_fusion.refs_0_.refs_2_, f32[1,1024]{1,0:T(1,128)S(1)} %get-tuple-element.174.refs_1_.refs_4_.refs_5_, f32[1,1024]{1,0:T(1,128)S(1)} %copy-done.64, ...), custom_call_target="tpu_custom_call" | custom-call | flops 2415919104 | bytes 17309696 | tf_op jit(solution)/shard_map/qkv_forward/pallas_call | solution.py:89
  48.6 17.8 %mlp_forward.3 = (f32[384,1024]{1,0:T(8,128)S(1)}, bf16[384,1024]{1,0:T(8,128)(2,1)S(1)}, bf16[1,384,4096]{2,1,0:T(8,128)(2,1)}, bf16[1,384,4096]{2,1,0:T(8,128)(2,1)}, bf16[384,1024]{1,0:T(8,128)(2,1)S(1)}) custom-call(s32[1]{0:T(128)} %bitcast.core_ref, f32[384,1024]{1,0:T(8,128)S(1)} %bitcast_add_fusion.refs_0_.refs_2_, bf16[384,1024]{1,0:T(8,128)(2,1)S(1)} %bitcast.84, ...), custom_call_target="tpu_custom_call" | custom-call | flops 7247757312 | bytes 49553408 | tf_op jit(solution)/shard_map/mlp_forward/pallas_call | solution.py:89
  94.0 20.8 %mlp_backward.2 = (bf16[1,384,2048]{2,1,0:T(8,128)(2,1)S(1)}, bf16[1,384,2048]{2,1,0:T(8,128)(2,1)S(1)}, f32[384,1024]{1,0:T(8,128)}, bf16[384,1024]{1,0:T(8,128...) custom-call(s32[1]{0:T(128)} %bitcast.core_ref, ...), custom_call_target="tpu_custom_call" | custom-call | flops 7247757312 | bytes 49557504 | tf_op jit(solution)/shard_map/mlp_backward/pallas_call | solution.py:89
  122.0 5.9 %weight_grad.20 = bf16[512,2048]{1,0:T(8,128)(2,1)} custom-call(s32[9]{0:T(128)S(1)} %pad_add_fusion.table_ref, bf16[3,384,1024]{2,1,0:T(8,128)(2,1)} %place_columns.2.refs_0_.refs_1_, bf16[3,384,1024]{2,1,0:T(8,128)(2,1)} %place_columns.2.refs_0_.refs_1_, bf16[3,384,1024]{2,1,0:T(8,128)(2,1)} %collective-permute-done.9.refs_2_.refs_3_.refs_1_, ...), custom_call_target="tpu_custom_call" | custom-call | flops 1610612736 | bytes 6029312 | tf_op jit(solution)/shard_map/weight_grad/pallas_call | solution.py:711
  133.1 7.1 %local_attn_backward.1 = (bf16[2,3,128,1024]{3,2,1,0:T(8,128)(2,1)S(1)}, bf16[2,3,128,1024]{3,2,1,0:T(8,128)(2,1)}) custom-call(s32[1]{0:T(128)} %bitcast.core_ref, bf16[3,128,3072]{2,1,0:T(8,128)(2,1)} %bitcast.70, bf16[3,128,3072]{2,1,0:T(8,128)(2,1)} %bitcast.71, bf16[3,128,3072]{2,1,0:T(8,128)(2,1)} %bitcast.72, bf16[3,128,1024]{2,1,0:T(8,128)(2,1)S(1)} %bitcast.92, ...), custom_call_target="tpu_custom_call" | custom-call | flops 1572864000 | bytes 6291456 | tf_op jit(solution)/shard_map/local_attn_backward/pallas_call | solution.py:475
  146.0 8.3 %qkv_backward.2 = (f32[384,1024]{1,0:T(8,128)S(1)}, bf16[128,1024]{1,0:T(8,128)(2,1)S(1)}, f32[1,1024]{1,0:T(1,128)S(1)}) custom-call(s32[1]{0:T(128)} %bitcast.core_ref, bf16[2,384,1024]{2,1,0:T(8,128)(2,1)S(1)} %bitcast.78, bf16[2,384,1024]{2,1,0:T(8,128)(2,1)} %bitcast.23.refs_1_, f32[384,1024]{1,0:T(8,128)} %copy-done.6, ...), custom_call_target="tpu_custom_call" | custom-call | flops 2415919104 | bytes 20721664 | tf_op jit(solution)/shard_map/qkv_backward/pallas_call | solution.py:89
  165.5 12.6 %weight_grad.22 = bf16[256,2048]{1,0:T(8,128)(2,1)} custom-call(s32[9]{0:T(128)S(1)} %pad_add_fusion.table_ref, bf16[3,384,1024]{2,1,0:T(8,128)(2,1)} %place_columns.2.refs_0_.refs_1_, bf16[3,384,1024]{2,1,0:T(8,128)(2,1)} %collective-permute-done.9.refs_2_.refs_3_.refs_1_, bf16[1,384,2048]{2,1,0:T(8,128)(2,1)S(1)} %get-tuple-element.96.refs_4_.refs_2_, ...), custom_call_target="tpu_custom_call" | custom-call | flops 805306368 | bytes 5636096 | tf_op jit(solution)/shard_map/weight_grad/pallas_call | solution.py:711
  178.1 5.6 %weight_grad.23 = bf16[512,2048]{1,0:T(8,128)(2,1)} custom-call(s32[9]{0:T(128)S(1)} %pad_add_fusion.table_ref, bf16[3,384,1024]{2,1,0:T(8,128)(2,1)} %place_columns.2.refs_0_.refs_1_, bf16[3,384,1024]{2,1,0:T(8,128)(2,1)} %place_columns.2.refs_0_.refs_1_, bf16[3,384,1024]{2,1,0:T(8,128)(2,1)} %collective-permute-done.9.refs_2_.refs_3_.refs_1_, ...), custom_call_target="tpu_custom_call" | custom-call | flops 1610612736 | bytes 6029312 | tf_op jit(solution)/shard_map/weight_grad/pallas_call | solution.py:711
  183.7 15.2 %mlp_backward.3 = (bf16[1,128,2048]{2,1,0:T(8,128)(2,1)S(1)}, bf16[1,128,2048]{2,1,0:T(8,128)(2,1)}, f32[128,1024]{1,0:T(8,128)S(1)}, bf16[128,1024]{1,0:T(8,128...) custom-call(s32[1]{0:T(128)} %bitcast.core_ref, bf16[128,1024]{1,0:T(8,128)(2,1)S(1)} %get-tuple-element.113.refs_0_, ...), custom_call_target="tpu_custom_call" | custom-call | flops 2415919104 | bytes 47984640 | tf_op jit(solution)/shard_map/mlp_backward/pallas_call | solution.py:89
  210.4 6.2 %global_attn_backward.1 = (bf16[2,128,1024]{2,1,0:T(8,128)(2,1)S(1)}, bf16[2,128,1024]{2,1,0:T(8,128)(2,1)}) custom-call(s32[1]{0:T(128)} %bitcast.core_ref, s32[2,1,8]{2,1,0:T(1,128)S(1)} %copy-done.65, bf16[7,256,1024]{2,1,0:T(8,128)(2,1)S(1)} %copy-done.2, bf16[7,256,1024]{2,1,0:T(8,128)(2,1)S(1)} %copy-done.2, bf16[7,256,1024]{2,1,0:T(8,128)(2,1)S(1)} %copy-done.2, ...), custom_call_target="tpu_custom_call" | custom-call | flops 524288000 | bytes 2097152 | tf_op jit(solution)/shard_map/global_attn_backward/pallas_call | solution.py:599
  219.2 6.4 %qkv_backward.3 = (f32[128,1024]{1,0:T(8,128)S(1)}, bf16[128,1024]{1,0:T(8,128)(2,1)}, f32[1,1024]{1,0:T(1,128)S(1)}) custom-call(s32[1]{0:T(128)} %bitcast.core_ref, bf16[2,128,1024]{2,1,0:T(8,128)(2,1)S(1)} %get-tuple-element.122.refs_0_.refs_2_.refs_1_, bf16[2,128,1024]{2,1,0:T(8,128)(2,1)} %get-tuple-element.126.refs_1_, f32[128,1024]{1,0:T(8,128)S(1)} %copy-done.31, ...), custom_call_target="tpu_custom_call" | custom-call | flops 805306368 | bytes 15478784 | tf_op jit(solution)/shard_map/qkv_backward/pallas_call | solution.py:89
  235.1 31.2 %collective-permute-done.46 = bf16[512,512]{1,0:T(8,128)(2,1)S(1)} collective-permute-done((bf16[512,512]{1,0:T(8,128)(2,1)S(1)}, bf16[512,512]{1,0:T(8,128)(2,1)S(1)}, u32[]{:S(2)}, u32[]{:S(2)}) %collective-permute-start.46) | collective-permute-done | bytes 524320 | tf_op jit(solution)/shard_map/ppermute | solution.py:747
  283.5 5.2 %collective-permute-done.25.refs_5_ = bf16[256,2048]{1,0:T(8,128)(2,1)} collective-permute-done((bf16[256,2048]{1,0:T(8,128)(2,1)}, bf16[256,2048]{1,0:T(8,128)(2,1)}, u32[]{:S(2)}, u32[]{:S(2)}) %collective-permute-start.25) | collective-permute-done | bytes 1048608 | tf_op jit(solution)/shard_map/ppermute | solution.py:747
  300.3 5.2 %collective-permute-start.31 = (bf16[1024,512]{1,0:T(8,128)(2,1)}, bf16[1024,512]{1,0:T(8,128)(2,1)}, u32[]{:S(2)}, u32[]{:S(2)}) collective-permute-start(bf16[1024,512]{1,0:T(8,128)(2,1)} %weight_grad.29), channel_id=1, source_target_pairs={{0,8},{1,9},{2,10},{3,11},{4,12},{5,13},{6,14},{7,15},{8,0},{9,1},... | collective-permute-start | bytes 3145736 | tf_op jit(solution)/shard_map/ppermute | solution.py:747
  328.1 28.6 %collective-permute-done.31.refs_7_ = bf16[1024,512]{1,0:T(8,128)(2,1)} collective-permute-done((bf16[1024,512]{1,0:T(8,128)(2,1)}, bf16[1024,512]{1,0:T(8,128)(2,1)}, u32[]{:S(2)}, u32[]{:S(2)}) %collective-permute-start.31) | collective-permute-done | bytes 1048608 | tf_op jit(solution)/shard_map/ppermute | solution.py:747
  372.2 13.3 %collective-permute-done.36 = bf16[128,2048]{1,0:T(8,128)(2,1)S(1)} collective-permute-done((bf16[128,2048]{1,0:T(8,128)(2,1)S(1)}, bf16[128,2048]{1,0:T(8,128)(2,1)S(1)}, u32[]{:S(2)}, u32[]{:S(2)}) %collective-permute-start.36) | collective-permute-done | bytes 524320 | tf_op jit(solution)/shard_map/ppermute | solution.py:747
  386.9 4.9 %collective-permute-done.45 = bf16[256,512]{1,0:T(8,128)(2,1)S(1)} collective-permute-done((bf16[256,512]{1,0:T(8,128)(2,1)S(1)}, bf16[256,512]{1,0:T(8,128)(2,1)S(1)}, u32[]{:S(2)}, u32[]{:S(2)}) %collective-permute-start.45) | collective-permute-done | bytes 262176 | tf_op jit(solution)/shard_map/ppermute | solution.py:747
  392.1 8.4 %collective-permute-done.39 = bf16[128,2048]{1,0:T(8,128)(2,1)S(1)} collective-permute-done((bf16[128,2048]{1,0:T(8,128)(2,1)S(1)}, bf16[128,2048]{1,0:T(8,128)(2,1)S(1)}, u32[]{:S(2)}, u32[]{:S(2)}) %collective-permute-start.39) | collective-permute-done | bytes 524320 | tf_op jit(solution)/shard_map/ppermute | solution.py:747
  408.1 5.8 %collective-permute-done.40 = bf16[64,2048]{1,0:T(8,128)(2,1)S(1)} collective-permute-done((bf16[64,2048]{1,0:T(8,128)(2,1)S(1)}, bf16[64,2048]{1,0:T(8,128)(2,1)S(1)}, u32[]{:S(2)}, u32[]{:S(2)}) %collective-permute-start.40) | collective-permute-done | bytes 262176 | tf_op jit(solution)/shard_map/ppermute | solution.py:747
  414.2 8.0 %collective-permute-done.34 = bf16[128,2048]{1,0:T(8,128)(2,1)S(1)} collective-permute-done((bf16[128,2048]{1,0:T(8,128)(2,1)S(1)}, bf16[128,2048]{1,0:T(8,128)(2,1)S(1)}, u32[]{:S(2)}, u32[]{:S(2)}) %collective-permute-start.34) | collective-permute-done | bytes 524320 | tf_op jit(solution)/shard_map/ppermute | solution.py:747
  422.8 11.9 %collective-permute-done.35 = bf16[64,2048]{1,0:T(8,128)(2,1)S(1)} collective-permute-done((bf16[64,2048]{1,0:T(8,128)(2,1)S(1)}, bf16[64,2048]{1,0:T(8,128)(2,1)S(1)}, u32[]{:S(2)}, u32[]{:S(2)}) %collective-permute-start.35) | collective-permute-done | bytes 262176 | tf_op jit(solution)/shard_map/ppermute | solution.py:747
  (334 shorter events, 176.5 us)
Async XLA Ops:
  0.6 47.9 %collective-permute-start.4 = (bf16[1024,4096]{1,0:T(8,128)(2,1)}, bf16[1024,4096]{1,0:T(8,128)(2,1)}, u32[]{:S(2)}, u32[]{:S(2)}) collective-permute-start(bf16[1024,4096]{1,0:T(8,128)(2,1)} %bitcast.94), channel_id=1, source_target_pairs={{0,16},{16,0},{1,17},{17,1},{2,18},{18,2},{3,19},{19,3},{4,20},{20... | collective-permute-start | bytes 25165832 | tf_op jit(solution)/shard_map/ppermute | solution.py:750
  1.1 47.4 %collective-permute-start.5 = (bf16[4096,1024]{1,0:T(8,128)(2,1)}, bf16[4096,1024]{1,0:T(8,128)(2,1)}, u32[]{:S(2)}, u32[]{:S(2)}) collective-permute-start(bf16[4096,1024]{1,0:T(8,128)(2,1)} %bitcast.99), channel_id=1, source_target_pairs={{0,16},{16,0},{1,17},{17,1},{2,18},{18,2},{3,19},{19,3},{4,20},{20... | collective-permute-start | bytes 25165832 | tf_op jit(solution)/shard_map/ppermute | solution.py:750
  1.2 37.5 %collective-permute-start.2 = (bf16[1024,3072]{1,0:T(8,128)(2,1)}, bf16[1024,3072]{1,0:T(8,128)(2,1)}, u32[]{:S(2)}, u32[]{:S(2)}) collective-permute-start(bf16[1024,3072]{1,0:T(8,128)(2,1)} %bitcast.104), channel_id=1, source_target_pairs={{0,16},{16,0},{1,17},{17,1},{2,18},{18,2},{3,19},{19,3},{4,20},{20... | collective-permute-start | bytes 18874376 | tf_op jit(solution)/shard_map/ppermute | solution.py:750
  1.7 46.8 %collective-permute-start.3 = (bf16[1024,1024]{1,0:T(8,128)(2,1)}, bf16[1024,1024]{1,0:T(8,128)(2,1)}, u32[]{:S(2)}, u32[]{:S(2)}) collective-permute-start(bf16[1024,1024]{1,0:T(8,128)(2,1)} %bitcast.73), channel_id=1, source_target_pairs={{0,16},{16,0},{1,17},{17,1},{2,18},{18,2},{3,19},{19,3},{4,20},{20... | collective-permute-start | bytes 6291464 | tf_op jit(solution)/shard_map/ppermute | solution.py:750
  2.5 30.9 %collective-permute-start.1 = (f32[2,1024]{1,0:T(2,128)S(1)}, f32[2,1024]{1,0:T(2,128)S(1)}, u32[]{:S(2)}, u32[]{:S(2)}) collective-permute-start(f32[2,1024]{1,0:T(2,128)S(1)} %pad_maximum_fusion.1), channel_id=1, source_target_pairs={{0,16},{16,0},{1,17},{17,1},{2,18},{18,2},{3,19},{19,3},{4,20},{20... | collective-permute-start | bytes 24584 | tf_op jit(solution)/shard_map/ppermute | solution.py:750
  71.6 58.3 %collective-permute-start.15 = (bf16[7,256,1024]{2,1,0:T(8,128)(2,1)}, bf16[7,256,1024]{2,1,0:T(8,128)(2,1)}, u32[]{:S(2)}, u32[]{:S(2)}) collective-permute-start(bf16[7,256,1024]{2,1,0:T(8,128)(2,1)} %pack.1), channel_id=1, source_target_pairs={{0,16},{1,17},{2,18},{3,19},{4,20},{5,21},{6,22},{7,23},{8,24},{9,... | collective-permute-start | bytes 11010056 | tf_op jit(solution)/shard_map/ppermute | solution.py:873
  75.3 66.1 %collective-permute-start.14 = (bf16[2,256,4096]{2,1,0:T(8,128)(2,1)}, bf16[2,256,4096]{2,1,0:T(8,128)(2,1)}, u32[]{:S(2)}, u32[]{:S(2)}) collective-permute-start(bf16[2,256,4096]{2,1,0:T(8,128)(2,1)} %get-tuple-element.114), channel_id=1, source_target_pairs={{0,16},{1,17},{2,18},{3,19},{4,20},{5,21},{6,22},{7,23},{8,24},{9,... | collective-permute-start | bytes 12582920 | tf_op jit(solution)/shard_map/ppermute | solution.py:873
  87.2 34.8 %collective-permute-start.9 = (bf16[3,384,1024]{2,1,0:T(8,128)(2,1)}, bf16[3,384,1024]{2,1,0:T(8,128)(2,1)}, u32[]{:S(2)}, u32[]{:S(2)}) collective-permute-start(bf16[3,384,1024]{2,1,0:T(8,128)(2,1)} %place_columns.2.refs_0_.refs_1_), channel_id=1, source_target_pairs={{0,16},{16,0},{1,17},{17,1},{2,18},{18,2},{3,19},{19,3},{4,20},{20... | collective-permute-start | bytes 7077896 | tf_op jit(solution)/shard_map/ppermute | solution.py:750
  127.9 37.6 %collective-permute-start.12 = (bf16[512,2048]{1,0:T(8,128)(2,1)}, bf16[512,2048]{1,0:T(8,128)(2,1)}, u32[]{:S(2)}, u32[]{:S(2)}) collective-permute-start(bf16[512,2048]{1,0:T(8,128)(2,1)} %weight_grad.20), channel_id=1, source_target_pairs={{0,1},{1,0},{2,3},{3,2},{4,5},{5,4},{6,7},{7,6},{8,9},{9,8},{10,11... | collective-permute-start | bytes 6291464 | tf_op jit(solution)/shard_map/ppermute | solution.py:747
  140.2 37.9 %collective-permute-start.13 = (bf16[2,384,1024]{2,1,0:T(8,128)(2,1)}, bf16[2,384,1024]{2,1,0:T(8,128)(2,1)S(1)}, u32[]{:S(2)}, u32[]{:S(2)}) collective-permute-start(bf16[2,384,1024]{2,1,0:T(8,128)(2,1)} %bitcast.23.refs_1_), channel_id=1, source_target_pairs={{0,16},{16,0},{1,17},{17,1},{2,18},{18,2},{3,19},{19,3},{4,20},{20... | collective-permute-start | bytes 4718600 | tf_op jit(solution)/shard_map/ppermute | solution.py:750
  201.4 90.8 %collective-permute-start.26 = (bf16[512,2048]{1,0:T(8,128)(2,1)}, bf16[512,2048]{1,0:T(8,128)(2,1)}, u32[]{:S(2)}, u32[]{:S(2)}) collective-permute-start(bf16[512,2048]{1,0:T(8,128)(2,1)} %weight_grad.23), channel_id=1, source_target_pairs={{0,1},{1,0},{2,3},{3,2},{4,5},{5,4},{6,7},{7,6},{8,9},{9,8},{10,11... | collective-permute-start | bytes 6291464 | tf_op jit(solution)/shard_map/ppermute | solution.py:747
  207.5 89.3 %collective-permute-start.27 = (bf16[2048,512]{1,0:T(8,128)(2,1)}, bf16[2048,512]{1,0:T(8,128)(2,1)}, u32[]{:S(2)}, u32[]{:S(2)}) collective-permute-start(bf16[2048,512]{1,0:T(8,128)(2,1)} %weight_grad.24), channel_id=1, source_target_pairs={{0,4},{1,5},{2,6},{3,7},{4,0},{5,1},{6,2},{7,3},{8,12},{9,13},{10,... | collective-permute-start | bytes 6291464 | tf_op jit(solution)/shard_map/ppermute | solution.py:747
  209.9 56.4 %collective-permute-start.46 = (bf16[512,512]{1,0:T(8,128)(2,1)S(1)}, bf16[512,512]{1,0:T(8,128)(2,1)S(1)}, u32[]{:S(2)}, u32[]{:S(2)}) collective-permute-start(bf16[512,512]{1,0:T(8,128)(2,1)S(1)} %copy-done.69), channel_id=1, source_target_pairs={{0,4},{1,5},{2,6},{3,7},{4,0},{5,1},{6,2},{7,3},{8,12},{9,13},{10,... | collective-permute-start | bytes 1572872 | tf_op jit(solution)/shard_map/ppermute | solution.py:747
  230.2 43.3 %collective-permute-start.24 = (bf16[2,128,1024]{2,1,0:T(8,128)(2,1)}, bf16[2,128,1024]{2,1,0:T(8,128)(2,1)}, u32[]{:S(2)}, u32[]{:S(2)}) collective-permute-start(bf16[2,128,1024]{2,1,0:T(8,128)(2,1)} %get-tuple-element.126.refs_1_), channel_id=1, source_target_pairs={{0,16},{16,0},{1,17},{17,1},{2,18},{18,2},{3,19},{19,3},{4,20},{20... | collective-permute-start | bytes 1572872 | tf_op jit(solution)/shard_map/ppermute | solution.py:750
  234.1 75.3 %collective-permute-start.28 = (bf16[512,2048]{1,0:T(8,128)(2,1)}, bf16[512,2048]{1,0:T(8,128)(2,1)}, u32[]{:S(2)}, u32[]{:S(2)}) collective-permute-start(bf16[512,2048]{1,0:T(8,128)(2,1)} %weight_grad.25), channel_id=1, source_target_pairs={{0,1},{1,0},{2,3},{3,2},{4,5},{5,4},{6,7},{7,6},{8,9},{9,8},{10,11... | collective-permute-start | bytes 6291464 | tf_op jit(solution)/shard_map/ppermute | solution.py:747
  280.9 44.7 %collective-permute-start.30 = (bf16[512,2048]{1,0:T(8,128)(2,1)}, bf16[512,2048]{1,0:T(8,128)(2,1)}, u32[]{:S(2)}, u32[]{:S(2)}) collective-permute-start(bf16[512,2048]{1,0:T(8,128)(2,1)} %weight_grad.26), channel_id=1, source_target_pairs={{0,1},{1,0},{2,3},{3,2},{4,5},{5,4},{6,7},{7,6},{8,9},{9,8},{10,11... | collective-permute-start | bytes 6291464 | tf_op jit(solution)/shard_map/ppermute | solution.py:747
  300.3 56.5 %collective-permute-start.31 = (bf16[1024,512]{1,0:T(8,128)(2,1)}, bf16[1024,512]{1,0:T(8,128)(2,1)}, u32[]{:S(2)}, u32[]{:S(2)}) collective-permute-start(bf16[1024,512]{1,0:T(8,128)(2,1)} %weight_grad.29), channel_id=1, source_target_pairs={{0,8},{1,9},{2,10},{3,11},{4,12},{5,13},{6,14},{7,15},{8,0},{9,1},... | collective-permute-start | bytes 3145736 | tf_op jit(solution)/shard_map/ppermute | solution.py:747
  314.0 54.5 %collective-permute-start.32 = (bf16[256,2048]{1,0:T(8,128)(2,1)S(1)}, bf16[256,2048]{1,0:T(8,128)(2,1)S(1)}, u32[]{:S(2)}, u32[]{:S(2)}) collective-permute-start(bf16[256,2048]{1,0:T(8,128)(2,1)S(1)} %weight_grad.30), channel_id=1, source_target_pairs={{0,2},{1,3},{2,0},{3,1},{4,6},{5,7},{6,4},{7,5},{8,10},{9,11},{10,... | collective-permute-start | bytes 3145736 | tf_op jit(solution)/shard_map/ppermute | solution.py:747
  315.3 49.7 %collective-permute-start.41 = (bf16[128,2048]{1,0:T(8,128)(2,1)S(1)}, bf16[128,2048]{1,0:T(8,128)(2,1)S(1)}, u32[]{:S(2)}, u32[]{:S(2)}) collective-permute-start(bf16[128,2048]{1,0:T(8,128)(2,1)S(1)} %copy-done.71), channel_id=1, source_target_pairs={{0,4},{1,5},{2,6},{3,7},{4,0},{5,1},{6,2},{7,3},{8,12},{9,13},{10,... | collective-permute-start | bytes 1572872 | tf_op jit(solution)/shard_map/ppermute | solution.py:747
  319.6 66.7 %collective-permute-start.47 = (bf16[256,512]{1,0:T(8,128)(2,1)S(1)}, bf16[256,512]{1,0:T(8,128)(2,1)S(1)}, u32[]{:S(2)}, u32[]{:S(2)}) collective-permute-start(bf16[256,512]{1,0:T(8,128)(2,1)S(1)} %copy-done.78), channel_id=1, source_target_pairs={{0,8},{1,9},{2,10},{3,11},{4,12},{5,13},{6,14},{7,15},{8,0},{9,1},... | collective-permute-start | bytes 786440 | tf_op jit(solution)/shard_map/ppermute | solution.py:747
  365.1 43.0 %collective-permute-start.42 = (bf16[64,2048]{1,0:T(8,128)(2,1)S(1)}, bf16[64,2048]{1,0:T(8,128)(2,1)S(1)}, u32[]{:S(2)}, u32[]{:S(2)}) collective-permute-start(bf16[64,2048]{1,0:T(8,128)(2,1)S(1)} %add_convert_fusion.2), channel_id=1, source_target_pairs={{0,8},{1,9},{2,10},{3,11},{4,12},{5,13},{6,14},{7,15},{8,0},{9,1},... | collective-permute-start | bytes 786440 | tf_op jit(solution)/shard_map/ppermute | solution.py:747
  368.5 33.3 %collective-permute-start.33 = (bf16[256,2048]{1,0:T(8,128)(2,1)S(1)}, bf16[256,2048]{1,0:T(8,128)(2,1)S(1)}, u32[]{:S(2)}, u32[]{:S(2)}) collective-permute-start(bf16[256,2048]{1,0:T(8,128)(2,1)S(1)} %weight_grad.32), channel_id=1, source_target_pairs={{0,2},{1,3},{2,0},{3,1},{4,6},{5,7},{6,4},{7,5},{8,10},{9,11},{10,... | collective-permute-start | bytes 3145736 | tf_op jit(solution)/shard_map/ppermute | solution.py:747
  372.1 28.5 %collective-permute-start.39 = (bf16[128,2048]{1,0:T(8,128)(2,1)S(1)}, bf16[128,2048]{1,0:T(8,128)(2,1)S(1)}, u32[]{:S(2)}, u32[]{:S(2)}) collective-permute-start(bf16[128,2048]{1,0:T(8,128)(2,1)S(1)} %get-tuple-element.150), channel_id=1, source_target_pairs={{0,4},{1,5},{2,6},{3,7},{4,0},{5,1},{6,2},{7,3},{8,12},{9,13},{10,... | collective-permute-start | bytes 1572872 | tf_op jit(solution)/shard_map/ppermute | solution.py:747
  386.4 36.4 %collective-permute-start.37 = (bf16[64,2048]{1,0:T(8,128)(2,1)S(1)}, bf16[64,2048]{1,0:T(8,128)(2,1)S(1)}, u32[]{:S(2)}, u32[]{:S(2)}) collective-permute-start(bf16[64,2048]{1,0:T(8,128)(2,1)S(1)} %add_convert_fusion.4), channel_id=1, source_target_pairs={{0,8},{1,9},{2,10},{3,11},{4,12},{5,13},{6,14},{7,15},{8,0},{9,1},... | collective-permute-start | bytes 786440 | tf_op jit(solution)/shard_map/ppermute | solution.py:747
  (109 other events, 1155.1 us)
